TPU v7x, 512 devices: a whole 4x8x8 slice. The times are simulated.
512 devices in a mesh: lon: 32 (over y_hi, z, core), lat: 16 (over y_lo, x).
Axes of the slice: x: 4, y: 8 (y_hi: 2, y_lo: 4; y = y_hi * 4 + y_lo), z: 8, core: 2. Of those that a mesh axis runs over, the one named last changes fastest.
Arguments:
- tracer_adjoint: bfloat16 [512, 64, 64, 128], P('lat', 'lon'), may hold values from -6 to 6
- tracer_old: bfloat16 [512, 64, 64, 128], P('lat', 'lon'), may hold values from -6 to 6
- owner_lon: int32 [512, 64], P('lat', 'lon'), may hold values from 0 to 31, as said below
- row_step: int32 [512, 64], P('lat', 'lon'), may hold values from 0 to 2
- owner_column: int32 [512, 64], P('lat', 'lon'), may hold values from 0 to 1
- tile_kind: int32 [512, 64], P('lat', 'lon'), may hold values from 0 to 3
- blend_weights: bfloat16 [4, 128, 128], replicated, may hold values from -0.5 to 0.5
- slope_east: bfloat16 [4, 128, 128], replicated, may hold values from -0.0625 to 0.0625
- slope_north: bfloat16 [4, 128, 128], replicated, may hold values from -0.0625 to 0.0625
Outputs:
- tracer_old_adjoint: bfloat16 [512, 64, 64, 128], P('lat', 'lon')
- wind_sensitivity: float32 [512, 64, 2, 128], P('lat', 'lon')
Inputs may be any that keep to these rules, and one draw needn't show every extreme that they name: `owner_lon`: A tile of longitude device h names h itself or a device h + d modulo 32 with 1 <= d <= 16 or 1 <= -d < 16, the reach growing from the equatorial row groups to the polar ones. Among the tiles of one device (rows 32 g to 32 g + 31, tile columns 2 h to 2 h + 1) at most 4 name any one longitude device other than h; for every group of 32 rows one other longitude device is named exactly 4 times by the tiles of every device of that group, in the two polar groups the device h + 16.
All inputs are finite; a program needn't handle non-finite values.
Results may differ from a plain program's by a relative error of at most 0.0075.
Values may be sent and summed in bfloat16 or wider, within the bound.
No kernel may reach another device: no remote copies, remote signals or barrier semaphores. Data moves between devices by JAX's collectives and lax.ppermute only.
A program may use at most 128 MiB of HBM per device.

v0:
```python
import jax
import jax.numpy as jnp
from jax import lax
from jax.sharding import PartitionSpec as P


def extended_2(shard, sides, width):
    for axis, dim in sides:
        count, length = (lax.axis_size(axis), shard.shape[dim])
        up = [(i, (i + 1) % count) for i in range(count - 1)]
        down = [(j, i) for i, j in up]
        last = lax.slice_in_dim(shard, length - width, length, axis=dim)
        initial = lax.slice_in_dim(shard, 0, width, axis=dim)
        before = lax.ppermute(last, axis, up)
        after = lax.ppermute(initial, axis, down)
        shard = jnp.concatenate([before, shard, after], axis=dim)
    return shard


def sensitivity(patches, adjoint_tiles, kind_index, slope_east, slope_north):
    east = jnp.einsum(
        "tlm,tma->tla", patches, slope_east[kind_index], preferred_element_type=jnp.float32
    )
    north = jnp.einsum(
        "tlm,tma->tla", patches, slope_north[kind_index], preferred_element_type=jnp.float32
    )
    adjoint_full = adjoint_tiles.astype(jnp.float32)
    return jnp.stack(
        [jnp.sum(adjoint_full * east, axis=1), jnp.sum(adjoint_full * north, axis=1)], axis=1
    )


def spread_back(adjoint_tiles, kind_index, blend_weights):
    product = jnp.einsum(
        "tla,tma->tlm", adjoint_tiles, blend_weights[kind_index], preferred_element_type=jnp.float32
    )
    return product.astype(jnp.bfloat16)


def on_device(
    tracer_adjoint,
    tracer_old,
    owner_lon,
    row_step,
    owner_column,
    tile_kind,
    blend_weights,
    slope_east,
    slope_north,
):
    lon_count = lax.axis_size("lon")
    own_column = lax.axis_index("lon")
    tile_rows, tile_cols = owner_lon.shape
    tiles_here = tile_rows * tile_cols
    capacity = max(2, (2 * tiles_here + lon_count - 1) // lon_count)
    levels = tracer_adjoint.shape[2]
    width = tracer_adjoint.shape[3]
    slot_count = lon_count * capacity
    block_count = (tile_rows + 2) * tile_cols
    target = owner_lon.reshape(tiles_here)
    at_home = target == own_column
    onehot = (
        (target[:, None] == jnp.arange(lon_count, dtype=jnp.int32)[None, :]) & (~at_home)[:, None]
    ).astype(jnp.int32)
    ranks = jnp.sum((jnp.cumsum(onehot, axis=0) - 1) * onehot, axis=1)
    places = jnp.where(at_home, slot_count, target * capacity + ranks)
    places_read = jnp.minimum(places, slot_count - 1)
    row_index = jnp.arange(tile_rows, dtype=jnp.int32)[:, None]
    extended = ((row_index + row_step) * tile_cols + owner_column).reshape(tiles_here)
    kind_here = tile_kind.reshape(tiles_here)
    rimmed = extended_2(tracer_old, (("lat", 0),), 1)
    source_blocks = rimmed.reshape(block_count, levels, width)
    adjoint_tiles = tracer_adjoint.reshape(tiles_here, levels, width)
    home_mask = at_home[:, None, None]
    request_slots = jnp.zeros((slot_count,), jnp.int32).at[places].set(extended, mode="drop")
    asked = lax.all_to_all(request_slots, "lon", split_axis=0, concat_axis=0, tiled=True)
    empty_slots = jnp.zeros((slot_count, levels, width), jnp.bfloat16)
    fetched = lax.all_to_all(source_blocks[asked], "lon", split_axis=0, concat_axis=0, tiled=True)
    patches = jnp.where(home_mask, source_blocks[extended], fetched[places_read])
    sensed = sensitivity(patches, adjoint_tiles, kind_here, slope_east, slope_north)
    spread = spread_back(adjoint_tiles, kind_here, blend_weights)
    returned = lax.all_to_all(
        empty_slots.at[places].set(spread, mode="drop"),
        "lon",
        split_axis=0,
        concat_axis=0,
        tiled=True,
    )
    summed = (
        jnp.zeros((block_count, levels, width), jnp.float32)
        .at[asked]
        .add(returned.astype(jnp.float32))
    )
    summed = summed.at[extended].add(jnp.where(home_mask, spread.astype(jnp.float32), 0.0))
    summed = summed.reshape(tile_rows + 2, tile_cols, levels, width)
    edges = jnp.stack([summed[0], summed[-1]], axis=0).astype(jnp.bfloat16)
    edged = extended_2(edges, (("lat", 0),), 1)
    interior = summed[1:-1]
    interior = interior.at[0].add(edged[0].astype(jnp.float32))
    interior = interior.at[-1].add(edged[3].astype(jnp.float32))
    return (interior.astype(jnp.bfloat16), sensed.reshape(tile_rows, tile_cols, 2, width))


def solution(mesh):
    return jax.shard_map(
        on_device,
        mesh=mesh,
        in_specs=(
            P("lat", "lon", None, None),
            P("lat", "lon", None, None),
            P("lat", "lon"),
            P("lat", "lon"),
            P("lat", "lon"),
            P("lat", "lon"),
            P(),
            P(),
            P(),
        ),
        out_specs=(P("lat", "lon", None, None), P("lat", "lon", None, None)),
        check_vma=False,
    )
```

profile of v0, /device:TPU:22, one launch (start us, length us, event | category | flops | bytes accessed | tf_op | source)
XLA Modules:
  0.0 183.8 jit_solution(2697240369595548840)
XLA Ops:
  0.6 0.8 copy.25
  1.4 0.7 broadcast_multiply_fusion
  2.2 0.7 broadcast_compare_fusion
  3.1 0.2 select_reduce_fusion
  3.3 0.1 copy.23
  3.4 0.1 eq.48
  3.6 0.1 mul.33
  3.7 0.8 copy.28
  4.5 0.1 reshape.263
  4.6 0.7 multiply_add_fusion
  5.4 0.1 reshape.320
  5.5 0.8 scatter_custom_fusion
  6.3 0.7 all_to_all.14
  7.0 14.2 %all-to-all-start = ((s32[32,4,1]{1,2,0:T(1,128)}), s32[32,4,1]{1,2,0:T(1,128)S(1)}, u32[]{:S(2)}, u32[]{:S(2)}) async-start(s32[32,4,1]{1,2,0:T(1,128)} %bitcast.2), calls=%async_computation | async-start | bytes 32768 | tf_op jit(solution)/shard_map/all_to_all | solution.py:76
  21.2 2.2 %gather_fusion = bf16[64,128,128]{2,1,0:T(8,128)(2,1)} fusion(bf16[4,128,128]{2,1,0:T(8,128)(2,1)S(1)} %copy-done, s32[1024]{0:T(1024)S(1)} %pad_clamp_fusion.3), kind=kCustom, calls=%fused_computation | custom fusion | bytes 4194560 | tf_op jit(solution)/shard_map/gather | solution.py:35
  23.4 4.5 %convert_select_fusion = (f32[64,64,128]{2,1,0:T(8,128)}, bf16[64,64,128]{2,1,0:T(8,128)(2,1)S(1)}) fusion(pred[64]{0:T(512)(128)(4,1)S(1)} %get-tuple-element.27, bf16[64,128,128]{2,1,0:T(8,128)(2,1)} %gather_fusion, bf16[64,64,128]{2,1,0:T(8,128)(2,1)S(1)} %bitcast.43), kind=kOutput, calls=%fused_computation.14 | convolution fusion | flops 135790592 | bytes 6291520 | tf_op jit(solution)/shard_map/tla,tma->tlm/dot_general | solution.py:34
  27.8 1.9 %broadcast_in_dim.24 = bf16[128,64,128]{2,1,0:T(8,128)(2,1)} broadcast(bf16[]{:T(256)} %constant.85.clone.1), dimensions={} | broadcast | bytes 2097154 | tf_op jit(solution)/shard_map/broadcast_in_dim | solution.py:77
  29.7 8.2 %scatter_fusion = bf16[128,64,128]{2,1,0:T(8,128)(2,1)} fusion(bf16[128,64,128]{2,1,0:T(8,128)(2,1)} %broadcast_in_dim.24, s32[64]{0:T(128)S(1)} %get-tuple-element.33, bf16[64,64,128]{2,1,0:T(8,128)(2,1)S(1)} %get-tuple-element.35), kind=kCustom, calls=%fused_computation.7 | custom fusion | bytes 3145984 | tf_op jit(solution)/shard_map/scatter | solution.py:83
  37.9 12.2 %all-to-all-start.1 = ((bf16[128,64,128]{2,1,0:T(8,128)(2,1)}), bf16[128,64,128]{2,1,0:T(8,128)(2,1)S(1)}, u32[]{:S(2)}, u32[]{:S(2)}) async-start(bf16[128,64,128]{2,1,0:T(8,128)(2,1)} %scatter_fusion), calls=%async_computation.1 | async-start | bytes 4194304 | tf_op jit(solution)/shard_map/all_to_all | solution.py:82
  50.2 0.8 fusion.17
  51.0 2.4 %collective-permute-start.2 = (bf16[1,2,64,128]{3,2,1,0:T(8,128)(2,1)S(1)}, bf16[1,2,64,128]{3,2,1,0:T(8,128)(2,1)S(1)}, u32[]{:S(2)}, u32[]{:S(2)}) collective-permute-start(bf16[1,2,64,128]{3,2,1,0:T(8,128)(2,1)S(1)} %get-tuple-element.30), channel_id=1, source_target_pairs={{0,1},{1,2},{2,3},{3,4},{4,5},{5,6},{6,7},{7,8},{8,9},{9,10},{10,1... | collective-permute-start | bytes 98312 | tf_op jit(solution)/shard_map/ppermute | solution.py:14
  53.4 3.4 %collective-permute-start.3 = (bf16[1,2,64,128]{3,2,1,0:T(8,128)(2,1)S(1)}, bf16[1,2,64,128]{3,2,1,0:T(8,128)(2,1)S(1)}, u32[]{:S(2)}, u32[]{:S(2)}) collective-permute-start(bf16[1,2,64,128]{3,2,1,0:T(8,128)(2,1)S(1)} %get-tuple-element.31), channel_id=1, source_target_pairs={{1,0},{2,1},{3,2},{4,3},{5,4},{6,5},{7,6},{8,7},{9,8},{10,9},{11,1... | collective-permute-start | bytes 98312 | tf_op jit(solution)/shard_map/ppermute | solution.py:15
  56.8 0.5 broadcast.232
  57.3 0.7 reduce.7
  58.0 0.1 all_to_all.16
  58.1 35.2 %collective-permute-done.2 = bf16[1,2,64,128]{3,2,1,0:T(8,128)(2,1)S(1)} collective-permute-done((bf16[1,2,64,128]{3,2,1,0:T(8,128)(2,1)S(1)}, bf16[1,2,64,128]{3,2,1,0:T(8,128)(2,1)S(1)}, u32[]{:S(2)}, u32[]{:S(2)}) %collective-permute-start.2) | collective-permute-done | bytes 32800 | tf_op jit(solution)/shard_map/ppermute | solution.py:14
  93.4 1.4 pad_maximum_fusion
  94.8 2.2 %gather_fusion.2 = bf16[128,64,128]{2,1,0:T(8,128)(2,1)} fusion(bf16[68,64,128]{2,1,0:T(8,128)(2,1)S(1)} %bitcast.41, s32[1024]{0:T(1024)S(1)} %pad_clamp_fusion.1), kind=kCustom, calls=%fused_computation.2 | custom fusion | bytes 4194816 | tf_op jit(solution)/shard_map/gather | solution.py:78
  96.9 7.4 %all-to-all-done.1 = bf16[128,64,128]{2,1,0:T(8,128)(2,1)S(1)} async-done(((bf16[128,64,128]{2,1,0:T(8,128)(2,1)}), bf16[128,64,128]{2,1,0:T(8,128)(2,1)S(1)}, u32[]{:S(2)}, u32[]{:S(2)}) %all-to-all-start.1) | async-done | bytes 2097184 | tf_op jit(solution)/shard_map/all_to_all | solution.py:82
  104.3 12.2 %all-to-all-start.2 = ((bf16[128,64,128]{2,1,0:T(8,128)(2,1)}), bf16[128,64,128]{2,1,0:T(8,128)(2,1)}, u32[]{:S(2)}, u32[]{:S(2)}) async-start(bf16[128,64,128]{2,1,0:T(8,128)(2,1)} %gather_fusion.2), calls=%async_computation.2 | async-start | bytes 4194304 | tf_op jit(solution)/shard_map/all_to_all | solution.py:78
  116.7 2.4 %convert_element_type.33 = f32[128,64,128]{2,1,0:T(8,128)} convert(bf16[128,64,128]{2,1,0:T(8,128)(2,1)S(1)} %all-to-all-done.1) | non-fusion elementwise | flops 1048576 | bytes 6291456 | tf_op jit(solution)/shard_map/convert_element_type | solution.py:92
  119.1 0.3 broadcast_in_dim.22
  119.3 13.6 %scatter_fusion.1 = f32[68,64,128]{2,1,0:T(8,128)S(1)} fusion(f32[68,64,128]{2,1,0:T(8,128)S(1)} %broadcast_in_dim.22, s32[128]{0:T(128)S(1)} %fusion.9, f32[128,64,128]{2,1,0:T(8,128)} %convert_element_type.33), kind=kCustom, calls=%fused_computation.8 | custom fusion | flops 1048576 | bytes 12583424 | tf_op jit(solution)/shard_map/scatter-add | solution.py:92
  132.9 7.0 %scatter_fusion.2 = f32[68,64,128]{2,1,0:T(8,128)S(1)} fusion(f32[68,64,128]{2,1,0:T(8,128)S(1)} %scatter_fusion.1, s32[64]{0:T(128)S(1)} %fusion.11, f32[64,64,128]{2,1,0:T(8,128)} %get-tuple-element.34), kind=kCustom, calls=%fused_computation.9 | custom fusion | flops 524288 | bytes 6291712 | tf_op jit(solution)/shard_map/scatter-add | solution.py:94
  139.9 0.2 convert.8
  140.2 1.9 %collective-permute-start = (bf16[1,2,64,128]{3,2,1,0:T(8,128)(2,1)S(1)}, bf16[1,2,64,128]{3,2,1,0:T(8,128)(2,1)S(1)}, u32[]{:S(2)}, u32[]{:S(2)}) collective-permute-start(bf16[1,2,64,128]{3,2,1,0:T(8,128)(2,1)S(1)} %get-tuple-element.29), channel_id=1, source_target_pairs={{0,1},{1,2},{2,3},{3,4},{4,5},{5,6},{6,7},{7,8},{8,9},{9,10},{10,1... | collective-permute-start | bytes 98312 | tf_op jit(solution)/shard_map/ppermute | solution.py:14
  142.1 2.1 %gather_fusion.4 = bf16[64,128,128]{2,1,0:T(8,128)(2,1)} fusion(bf16[4,128,128]{2,1,0:T(8,128)(2,1)S(1)} %copy-done.1, s32[1024]{0:T(1024)S(1)} %pad_clamp_fusion.3), kind=kCustom, calls=%fused_computation.4 | custom fusion | bytes 4194560 | tf_op jit(solution)/shard_map/gather | solution.py:22
  144.2 2.2 %gather_fusion.5 = bf16[64,128,128]{2,1,0:T(8,128)(2,1)} fusion(bf16[4,128,128]{2,1,0:T(8,128)(2,1)S(1)} %copy-done.2, s32[1024]{0:T(1024)S(1)} %pad_clamp_fusion.3), kind=kCustom, calls=%fused_computation.5 | custom fusion | bytes 4194560 | tf_op jit(solution)/shard_map/gather | solution.py:25
  146.4 2.0 %gather_fusion.1 = bf16[64,64,128]{2,1,0:T(8,128)(2,1)S(1)} fusion(bf16[68,64,128]{2,1,0:T(8,128)(2,1)} %bitcast.42, s32[1024]{0:T(1024)S(1)} %pad_clamp_fusion.2), kind=kCustom, calls=%fused_computation.1 | custom fusion | bytes 2097408 | tf_op jit(solution)/shard_map/gather | solution.py:79
  148.4 0.2 slice.106
  148.7 3.9 %collective-permute-start.1 = (bf16[1,2,64,128]{3,2,1,0:T(8,128)(2,1)S(1)}, bf16[1,2,64,128]{3,2,1,0:T(8,128)(2,1)S(1)}, u32[]{:S(2)}, u32[]{:S(2)}) collective-permute-start(bf16[1,2,64,128]{3,2,1,0:T(8,128)(2,1)S(1)} %get-tuple-element.28), channel_id=1, source_target_pairs={{1,0},{2,1},{3,2},{4,3},{5,4},{6,5},{7,6},{8,7},{9,8},{10,9},{11,1... | collective-permute-start | bytes 98312 | tf_op jit(solution)/shard_map/ppermute | solution.py:15
  152.6 18.6 %collective-permute-done = bf16[1,2,64,128]{3,2,1,0:T(8,128)(2,1)S(1)} collective-permute-done((bf16[1,2,64,128]{3,2,1,0:T(8,128)(2,1)S(1)}, bf16[1,2,64,128]{3,2,1,0:T(8,128)(2,1)S(1)}, u32[]{:S(2)}, u32[]{:S(2)}) %collective-permute-start) | collective-permute-done | bytes 32800 | tf_op jit(solution)/shard_map/ppermute | solution.py:14
  171.2 1.2 convert_element_type.37
  172.4 5.1 %all-to-all-done.2 = bf16[128,64,128]{2,1,0:T(8,128)(2,1)} async-done(((bf16[128,64,128]{2,1,0:T(8,128)(2,1)}), bf16[128,64,128]{2,1,0:T(8,128)(2,1)}, u32[]{:S(2)}, u32[]{:S(2)}) %all-to-all-start.2) | async-done | bytes 2097184 | tf_op jit(solution)/shard_map/all_to_all | solution.py:78
  177.5 2.3 %gather_fusion.3 = bf16[64,64,128]{2,1,0:T(8,128)(2,1)S(1)} fusion(bf16[128,64,128]{2,1,0:T(8,128)(2,1)} %all-to-all-done.2, s32[1024]{0:T(1024)S(1)} %pad_clamp_fusion), kind=kCustom, calls=%fused_computation.3 | custom fusion | bytes 2097408 | tf_op jit(solution)/shard_map/gather | solution.py:79
  179.8 2.5 %fusion = f32[64,128]{1,0:T(8,128)S(1)} fusion(bf16[64,64,128]{2,1,0:T(8,128)(2,1)S(1)} %bitcast.44, bf16[64,128,128]{2,1,0:T(8,128)(2,1)} %gather_fusion.4, bf16[64,64,128]{2,1,0:T(8,128)(2,1)S(1)} %gather_fusion.1, bf16[64,64,128]{2,1,0:T(8,128)(2,1)S(1)} %gather_fusion.3, pred[64]{0:T(512)(128)(4,1)S(1)} %get-tuple-element.27), kind=kOutput, calls=%fused_computation.12 | convolution fusion | flops 136306688 | bytes 5275712 | tf_op jit(solution)/shard_map/tlm,tma->tla/dot_general | solution.py:21
  182.4 0.8 fusion.1
  183.1 0.7 pad_maximum_fusion.1
  (34 shorter events, 0.7 us)
Async XLA Ops:
  0.6 20.6 %copy-start = (bf16[4,128,128]{2,1,0:T(8,128)(2,1)S(1)}, bf16[4,128,128]{2,1,0:T(8,128)(2,1)}, u32[]{:S(2)}) copy-start(bf16[4,128,128]{2,1,0:T(8,128)(2,1)} %param.19) | copy-start | bytes 393220
  7.0 30.9 %all-to-all-start = ((s32[32,4,1]{1,2,0:T(1,128)}), s32[32,4,1]{1,2,0:T(1,128)S(1)}, u32[]{:S(2)}, u32[]{:S(2)}) async-start(s32[32,4,1]{1,2,0:T(1,128)} %bitcast.2), calls=%async_computation | async-start | bytes 32768 | tf_op jit(solution)/shard_map/all_to_all | solution.py:76
  21.2 2.2 %copy-start.4 = (bf16[32,2,64,128]{3,2,1,0:T(8,128)(2,1)S(1)}, bf16[32,2,64,128]{3,2,1,0:T(8,128)(2,1)}, u32[]{:S(2)}) copy-start(bf16[32,2,64,128]{3,2,1,0:T(8,128)(2,1)} %param.13) | copy-start | bytes 3145732
  37.9 66.4 %all-to-all-start.1 = ((bf16[128,64,128]{2,1,0:T(8,128)(2,1)}), bf16[128,64,128]{2,1,0:T(8,128)(2,1)S(1)}, u32[]{:S(2)}, u32[]{:S(2)}) async-start(bf16[128,64,128]{2,1,0:T(8,128)(2,1)} %scatter_fusion), calls=%async_computation.1 | async-start | bytes 4194304 | tf_op jit(solution)/shard_map/all_to_all | solution.py:82
  51.0 42.4 %collective-permute-start.2 = (bf16[1,2,64,128]{3,2,1,0:T(8,128)(2,1)S(1)}, bf16[1,2,64,128]{3,2,1,0:T(8,128)(2,1)S(1)}, u32[]{:S(2)}, u32[]{:S(2)}) collective-permute-start(bf16[1,2,64,128]{3,2,1,0:T(8,128)(2,1)S(1)} %get-tuple-element.30), channel_id=1, source_target_pairs={{0,1},{1,2},{2,3},{3,4},{4,5},{5,6},{6,7},{7,8},{8,9},{9,10},{10,1... | collective-permute-start | bytes 98312 | tf_op jit(solution)/shard_map/ppermute | solution.py:14
  53.4 40.0 %collective-permute-start.3 = (bf16[1,2,64,128]{3,2,1,0:T(8,128)(2,1)S(1)}, bf16[1,2,64,128]{3,2,1,0:T(8,128)(2,1)S(1)}, u32[]{:S(2)}, u32[]{:S(2)}) collective-permute-start(bf16[1,2,64,128]{3,2,1,0:T(8,128)(2,1)S(1)} %get-tuple-element.31), channel_id=1, source_target_pairs={{1,0},{2,1},{3,2},{4,3},{5,4},{6,5},{7,6},{8,7},{9,8},{10,9},{11,1... | collective-permute-start | bytes 98312 | tf_op jit(solution)/shard_map/ppermute | solution.py:15
  94.8 2.2 %copy-start.3 = (bf16[34,2,64,128]{3,2,1,0:T(8,128)(2,1)}, bf16[34,2,64,128]{3,2,1,0:T(8,128)(2,1)S(1)}, u32[]{:S(2)}) copy-start(bf16[34,2,64,128]{3,2,1,0:T(8,128)(2,1)S(1)} %pad_maximum_fusion) | copy-start | bytes 3342340
  104.3 73.2 %all-to-all-start.2 = ((bf16[128,64,128]{2,1,0:T(8,128)(2,1)}), bf16[128,64,128]{2,1,0:T(8,128)(2,1)}, u32[]{:S(2)}, u32[]{:S(2)}) async-start(bf16[128,64,128]{2,1,0:T(8,128)(2,1)} %gather_fusion.2), calls=%async_computation.2 | async-start | bytes 4194304 | tf_op jit(solution)/shard_map/all_to_all | solution.py:78
  139.9 2.2 %copy-start.1 = (bf16[4,128,128]{2,1,0:T(8,128)(2,1)S(1)}, bf16[4,128,128]{2,1,0:T(8,128)(2,1)}, u32[]{:S(2)}) copy-start(bf16[4,128,128]{2,1,0:T(8,128)(2,1)} %param.20) | copy-start | bytes 393220
  140.2 31.0 %collective-permute-start = (bf16[1,2,64,128]{3,2,1,0:T(8,128)(2,1)S(1)}, bf16[1,2,64,128]{3,2,1,0:T(8,128)(2,1)S(1)}, u32[]{:S(2)}, u32[]{:S(2)}) collective-permute-start(bf16[1,2,64,128]{3,2,1,0:T(8,128)(2,1)S(1)} %get-tuple-element.29), channel_id=1, source_target_pairs={{0,1},{1,2},{2,3},{3,4},{4,5},{5,6},{6,7},{7,8},{8,9},{9,10},{10,1... | collective-permute-start | bytes 98312 | tf_op jit(solution)/shard_map/ppermute | solution.py:14
  142.1 2.1 %copy-start.2 = (bf16[4,128,128]{2,1,0:T(8,128)(2,1)S(1)}, bf16[4,128,128]{2,1,0:T(8,128)(2,1)}, u32[]{:S(2)}) copy-start(bf16[4,128,128]{2,1,0:T(8,128)(2,1)} %param.21) | copy-start | bytes 393220
  148.7 22.5 %collective-permute-start.1 = (bf16[1,2,64,128]{3,2,1,0:T(8,128)(2,1)S(1)}, bf16[1,2,64,128]{3,2,1,0:T(8,128)(2,1)S(1)}, u32[]{:S(2)}, u32[]{:S(2)}) collective-permute-start(bf16[1,2,64,128]{3,2,1,0:T(8,128)(2,1)S(1)} %get-tuple-element.28), channel_id=1, source_target_pairs={{1,0},{2,1},{3,2},{4,3},{5,4},{6,5},{7,6},{8,7},{9,8},{10,9},{11,1... | collective-permute-start | bytes 98312 | tf_op jit(solution)/shard_map/ppermute | solution.py:15
  171.2 8.6 %copy-start.5 = (bf16[32,2,64,128]{3,2,1,0:T(8,128)(2,1)S(1)}, bf16[32,2,64,128]{3,2,1,0:T(8,128)(2,1)}, u32[]{:S(2)}) copy-start(bf16[32,2,64,128]{3,2,1,0:T(8,128)(2,1)} %param.13) | copy-start | bytes 3145732
  179.8 2.5 %copy-start.6 = (bf16[64,128,128]{2,1,0:T(8,128)(2,1)S(1)}, bf16[64,128,128]{2,1,0:T(8,128)(2,1)}, u32[]{:S(2)}) copy-start(bf16[64,128,128]{2,1,0:T(8,128)(2,1)} %gather_fusion.5) | copy-start | bytes 6291460
where the time goes:
time: 185 us; the launch traced here: 184 us
  waiting for transfers between devices  66.3 us (36%)
  starting transfers between devices  50.3 us (27%)
  other arithmetic  29.6 us (16%)
  local copies, waits for them, and re-layouts  28.9 us (16%)
  matrix products  7.73 us (4%)
    ppermute x2, waiting for transfers between devices, extended_2(): before = lax.ppermute(last, axis, up)  53.8 us
    all_to_all x1, starting transfers between devices, on_device(): lax.all_to_all(request_slots, 'lon', split_axis=0, concat_axis=0, tiled=T...  14.2 us
    scatter-add x1, other arithmetic, on_device(): summed = jnp.zeros((block_count, levels, width), jnp.float32).at[asked].a...  13.6 us
    all_to_all x1, starting transfers between devices, on_device(): lax.all_to_all(source_blocks[asked], 'lon', split_axis=0, concat_axis=0,...  12.2 us
    all_to_all x1, starting transfers between devices, on_device(): lax.all_to_all(empty_slots.at[places].set(spread, mode='drop'), 'lon', sp...  12.2 us
    scatter x1, local copies, waits for them, and re-layouts, on_device(): empty_slots.at[places].set(spread, mode='drop')  8.21 us
    all_to_all x1, waiting for transfers between devices, on_device(): lax.all_to_all(empty_slots.at[places].set(spread, mode='drop'), 'lon', sp...  7.36 us
    ppermute x2, starting transfers between devices, extended_2(): after = lax.ppermute(initial, axis, down)  7.36 us
  transfers between devices with their start and end apart: 7, of which 4 were waited for; matrix products, arithmetic and copies ran while one was open for 29% of the time, Pallas kernels for 0%

commit v1 on v0

v1 whole, which is shorter than its diff:
```python
import functools

import jax
import jax.numpy as jnp
from jax import lax
from jax.experimental import pallas as pl
from jax.experimental.pallas import tpu as pltpu
from jax.sharding import PartitionSpec as P

CAP = 4
UNROLL = 4
KINDS = 4


def pack_kernel(owner, step, column, kind, adjoint, send, places, codes, counts, tiles, load_sem, sem):
    tile_cols, tile_rows = owner.shape
    tiles_here, levels, _ = adjoint.shape
    lon_count = counts.shape[0]
    me = lax.axis_index("lon")
    load = pltpu.make_async_copy(adjoint, tiles, load_sem)
    load.start()

    for d in range(lon_count):
        counts[d] = 0
        for r in range(CAP):
            codes[d * CAP + r] = 0

    def place_row(i, sent):
        for j in range(tile_cols):
            to = owner[j, i]
            rank = counts[to]
            counts[to] = rank + 1
            block = (i + step[j, i]) * tile_cols + column[j, i]
            code = block * KINDS + kind[j, i] + 1
            remote = to != me
            slot = jnp.where(remote, to * CAP + rank, lon_count * CAP)
            codes[slot] = code
            places[i * tile_cols + j] = jnp.where(remote, slot, -code)
            sent = sent + remote.astype(jnp.int32)
        return sent

    sent = lax.fori_loop(0, tile_rows, place_row, 0)
    load.wait()

    def send_row(i, carry):
        for j in range(tile_cols):
            tile = i * tile_cols + j
            slot = places[tile]

            @pl.when(slot >= 0)
            def _():
                pltpu.make_async_copy(tiles.at[tile], send.at[slot], sem).start()

        return carry

    lax.fori_loop(0, tile_rows, send_row, 0)

    def settle(_, carry):
        pltpu.make_async_copy(tiles.at[0], send.at[0], sem).wait()
        return carry

    lax.fori_loop(0, sent, settle, 0)


def pack(owner, step, column, kind, adjoint, lon_count):
    tiles_here, levels, width = adjoint.shape
    smem = pl.BlockSpec(memory_space=pltpu.SMEM)
    hbm = pl.BlockSpec(memory_space=pltpu.HBM)
    return pl.pallas_call(
        pack_kernel,
        out_shape=(
            jax.ShapeDtypeStruct((lon_count * CAP, levels, width), jnp.bfloat16),
            jax.ShapeDtypeStruct((tiles_here,), jnp.int32),
            jax.ShapeDtypeStruct((lon_count * CAP + 128,), jnp.int32),
        ),
        in_specs=[smem, smem, smem, smem, hbm],
        out_specs=(hbm, smem, smem),
        scratch_shapes=[
            pltpu.SMEM((lon_count,), jnp.int32),
            pltpu.VMEM((tiles_here, levels, width), jnp.bfloat16),
            pltpu.SemaphoreType.DMA,
            pltpu.SemaphoreType.DMA,
        ],
        name="pack",
    )(owner, step, column, kind, adjoint)


def adjoint_kernel(
    places, codes, received, adjoint, old, before, after, blend, east, north,
    result, edge_own, cross_before, cross_after, sensed_remote, sensed_home,
    tiles, sources, sums, sensed, back, slopes, work, sem, out_sem,
):
    tiles_here, levels, width = adjoint.shape
    slot_count = received.shape[0]
    tile_cols = before.shape[0]
    block_count = tiles_here + 2 * tile_cols

    loads = [
        pltpu.make_async_copy(received, tiles.at[pl.ds(0, slot_count)], sem.at[0]),
        pltpu.make_async_copy(adjoint, tiles.at[pl.ds(slot_count, tiles_here)], sem.at[1]),
        pltpu.make_async_copy(old, sources.at[pl.ds(tile_cols, tiles_here)], sem.at[2]),
        pltpu.make_async_copy(before, sources.at[pl.ds(0, tile_cols)], sem.at[3]),
        pltpu.make_async_copy(after, sources.at[pl.ds(tile_cols + tiles_here, tile_cols)], sem.at[4]),
    ]
    for copy in loads:
        copy.start()

    def enlist(n, count):
        for u in range(8):
            s = n * 8 + u
            code = codes[s]
            work[count] = s * 512 + code - 1
            count = count + (code > 0).astype(jnp.int32)
        return count

    count = lax.fori_loop(0, slot_count // 8, enlist, 0)

    def enlist_home(n, count):
        for u in range(8):
            t = n * 8 + u
            place = places[t]
            work[count] = (slot_count + t) * 512 - place - 1
            count = count + (place < 0).astype(jnp.int32)
        return count

    count = lax.fori_loop(0, tiles_here // 8, enlist_home, count)
    for u in range(UNROLL):
        work[count + u] = (slot_count + tiles_here) * 512 + block_count * KINDS

    for k in range(KINDS):
        back[k] = blend[k].T
        slopes[k, :, :width] = east[k]
        slopes[k, :, width:] = north[k]
    sources[block_count] = jnp.zeros((levels, width), jnp.bfloat16)
    tiles[slot_count + tiles_here] = jnp.zeros((levels, width), jnp.bfloat16)

    def clear(b, carry):
        sums[b] = jnp.zeros((levels, width), jnp.float32)
        return carry

    lax.fori_loop(0, block_count + 1, clear, 0, unroll=3)
    for copy in loads:
        copy.wait()

    def some_tiles(n, carry):
        entries = [work[n * UNROLL + u] for u in range(UNROLL)]
        place = [e >> 9 for e in entries]
        kind = [e & (KINDS - 1) for e in entries]
        block = [(e & 511) >> 2 for e in entries]
        arrived = [tiles[p] for p in place]
        spread = [
            jnp.dot(a, back[k], preferred_element_type=jnp.float32) for a, k in zip(arrived, kind)
        ]
        slope = [
            jnp.dot(sources[b], slopes[k], preferred_element_type=jnp.float32) for b, k in zip(block, kind)
        ]
        for p, a, s in zip(place, arrived, slope):
            full = a.astype(jnp.float32)
            sensed[p, 0:1] = jnp.sum(full * s[:, :width], axis=0, keepdims=True)
            sensed[p, 1:2] = jnp.sum(full * s[:, width:], axis=0, keepdims=True)
        for b, s in zip(block, spread):
            sums[b] += s.astype(jnp.bfloat16).astype(jnp.float32)
        return carry

    lax.fori_loop(0, (count + UNROLL - 1) // UNROLL, some_tiles, 0)

    outs = [
        pltpu.make_async_copy(sensed.at[pl.ds(0, slot_count)], sensed_remote, out_sem.at[0]),
        pltpu.make_async_copy(sensed.at[pl.ds(slot_count, tiles_here)], sensed_home, out_sem.at[1]),
    ]
    for copy in outs:
        copy.start()
    for c in range(tile_cols):
        cross_before[c] = sums[c].astype(jnp.bfloat16)
        cross_after[c] = sums[tile_cols + tiles_here + c].astype(jnp.bfloat16)
        edge_own[c] = sums[tile_cols + c]
        edge_own[tile_cols + c] = sums[tiles_here + c]

    def finish(b, carry):
        result[b] = sums[tile_cols + b].astype(jnp.bfloat16)
        return carry

    lax.fori_loop(0, tiles_here, finish, 0, unroll=4)
    for copy in outs:
        copy.wait()


def adjoint_step(places, codes, received, adjoint, old, before, after, blend, east, north):
    slot_count = received.shape[0]
    tiles_here, levels, width = adjoint.shape
    tile_cols = before.shape[0]
    block_count = tiles_here + 2 * tile_cols
    smem = pl.BlockSpec(memory_space=pltpu.SMEM)
    vmem = pl.BlockSpec(memory_space=pltpu.VMEM)
    hbm = pl.BlockSpec(memory_space=pltpu.HBM)
    edge = jax.ShapeDtypeStruct((tile_cols, levels, width), jnp.bfloat16)
    return pl.pallas_call(
        adjoint_kernel,
        out_shape=(
            jax.ShapeDtypeStruct((tiles_here, levels, width), jnp.bfloat16),
            jax.ShapeDtypeStruct((2 * tile_cols, levels, width), jnp.float32),
            edge,
            edge,
            jax.ShapeDtypeStruct((slot_count, 2, width), jnp.float32),
            jax.ShapeDtypeStruct((tiles_here, 2, width), jnp.float32),
        ),
        in_specs=[smem, smem, hbm, hbm, hbm, hbm, hbm, vmem, vmem, vmem],
        out_specs=(vmem, vmem, vmem, vmem, hbm, hbm),
        scratch_shapes=[
            pltpu.VMEM((slot_count + tiles_here + 1, levels, width), jnp.bfloat16),
            pltpu.VMEM((block_count + 1, levels, width), jnp.bfloat16),
            pltpu.VMEM((block_count + 1, levels, width), jnp.float32),
            pltpu.VMEM((slot_count + tiles_here + 1, 2, width), jnp.float32),
            pltpu.VMEM((KINDS, width, width), jnp.bfloat16),
            pltpu.VMEM((KINDS, width, 2 * width), jnp.bfloat16),
            pltpu.SMEM((slot_count + tiles_here + UNROLL,), jnp.int32),
            pltpu.SemaphoreType.DMA((5,)),
            pltpu.SemaphoreType.DMA((2,)),
        ],
        compiler_params=pltpu.CompilerParams(vmem_limit_bytes=32 * 1024 * 1024),
        name="adjoint",
    )(places, codes, received, adjoint, old, before, after, blend, east, north)


def finish_kernel(places, returned, sensed_home, edge_own, from_before, from_after, _, result, sensed, edges, sem):
    tiles_here = sensed.shape[0]
    tile_cols = from_before.shape[0]
    for c in range(tile_cols):
        edges[c] = (edge_own[c] + from_before[c].astype(jnp.float32)).astype(jnp.bfloat16)
        edges[tile_cols + c] = (edge_own[tile_cols + c] + from_after[c].astype(jnp.float32)).astype(jnp.bfloat16)
    copies = [
        pltpu.make_async_copy(edges.at[pl.ds(0, tile_cols)], result.at[pl.ds(0, tile_cols)], sem.at[0]),
        pltpu.make_async_copy(
            edges.at[pl.ds(tile_cols, tile_cols)], result.at[pl.ds(tiles_here - tile_cols, tile_cols)], sem.at[1]
        ),
    ]
    for copy in copies:
        copy.start()

    def place_one(t, carry):
        place = places[t]
        sensed[t] = jnp.where(place < 0, sensed_home[t], returned[jnp.maximum(place, 0)])
        return carry

    lax.fori_loop(0, tiles_here, place_one, 0)
    for copy in copies:
        copy.wait()


def finish(places, returned, sensed_home, edge_own, from_before, from_after, partial):
    tiles_here, _, width = sensed_home.shape
    smem = pl.BlockSpec(memory_space=pltpu.SMEM)
    vmem = pl.BlockSpec(memory_space=pltpu.VMEM)
    hbm = pl.BlockSpec(memory_space=pl.ANY)
    return pl.pallas_call(
        finish_kernel,
        out_shape=(
            jax.ShapeDtypeStruct(partial.shape, partial.dtype),
            jax.ShapeDtypeStruct((tiles_here, 2, width), jnp.float32),
        ),
        in_specs=[smem, vmem, vmem, vmem, vmem, vmem, hbm],
        out_specs=(hbm, vmem),
        scratch_shapes=[
            pltpu.VMEM(edge_own.shape, jnp.bfloat16),
            pltpu.SemaphoreType.DMA((2,)),
        ],
        input_output_aliases={6: 0},
        name="finish",
    )(places, returned, sensed_home, edge_own, from_before, from_after, partial)


def on_device(
    tracer_adjoint, tracer_old, owner_lon, row_step, owner_column, tile_kind, blend_weights, slope_east, slope_north
):
    lon_count = lax.axis_size("lon")
    lat_count = lax.axis_size("lat")
    tile_rows, tile_cols = owner_lon.shape
    levels, width = tracer_adjoint.shape[2:]
    tiles_here = tile_rows * tile_cols
    north_to_south = [(i, i + 1) for i in range(lat_count - 1)]
    south_to_north = [(j, i) for i, j in north_to_south]
    adjoint = tracer_adjoint.reshape(tiles_here, levels, width)
    old = tracer_old.reshape(tiles_here, levels, width)

    send, places, codes = pack(owner_lon.T, row_step.T, owner_column.T, tile_kind.T, adjoint, lon_count)
    received = lax.all_to_all(send, "lon", split_axis=0, concat_axis=0, tiled=True)
    before = lax.ppermute(old[-tile_cols:], "lat", north_to_south)
    after = lax.ppermute(old[:tile_cols], "lat", south_to_north)
    asked = lax.all_to_all(codes[: lon_count * CAP], "lon", split_axis=0, concat_axis=0, tiled=True)
    partial, edge_own, cross_before, cross_after, sensed_remote, sensed_home = adjoint_step(
        places, asked, received, adjoint, old, before, after, blend_weights, slope_east, slope_north
    )
    returned = lax.all_to_all(sensed_remote, "lon", split_axis=0, concat_axis=0, tiled=True)
    from_after = lax.ppermute(cross_before, "lat", south_to_north)
    from_before = lax.ppermute(cross_after, "lat", north_to_south)
    result, sensed = finish(places, returned, sensed_home, edge_own, from_before, from_after, partial)
    return (
        result.reshape(tracer_old.shape),
        sensed.reshape(tile_rows, tile_cols, 2, width),
    )


def solution(mesh):
    return jax.shard_map(
        on_device,
        mesh=mesh,
        in_specs=(
            P("lat", "lon", None, None),
            P("lat", "lon", None, None),
            P("lat", "lon"),
            P("lat", "lon"),
            P("lat", "lon"),
            P("lat", "lon"),
            P(),
            P(),
            P(),
        ),
        out_specs=(P("lat", "lon", None, None), P("lat", "lon", None, None)),
        check_vma=False,
    )
```

time: 185 us -> 130 us (0.70)
  the two profiles are of different devices: /device:TPU:22 before, /device:TPU:12 now
where the time goes in v1:
time: 130 us; the launch traced here: 129 us
  waiting for transfers between devices  55.1 us (42%)
  blocking collectives  27.1 us (21%)
  starting transfers between devices  22.9 us (18%)
  Pallas kernels  12.5 us (10%)
  local copies, waits for them, and re-layouts  8.6 us (7%)
  other arithmetic  2.04 us (2%)
    all_to_all x1, waiting for transfers between devices, on_device(): lax.all_to_all(send, 'lon', split_axis=0, concat_axis=0, tiled=True)  47 us
    all_to_all x1, blocking collectives, on_device(): lax.all_to_all(codes[:lon_count * CAP], 'lon', split_axis=0, concat_axis=...  27.1 us
    all_to_all x1, starting transfers between devices, on_device(): lax.all_to_all(sensed_remote, 'lon', split_axis=0, concat_axis=0, tiled=T...  7.11 us
    pallas_call x1, Pallas kernels, adjoint_step(): pl.pallas_call(adjoint_kernel, out_shape=(jax.ShapeDtypeStruct((tiles_her...  6.89 us
    unnamed x28, local copies, waits for them, and re-layouts  5.02 us
    all_to_all x1, waiting for transfers between devices, on_device(): lax.all_to_all(sensed_remote, 'lon', split_axis=0, concat_axis=0, tiled=T...  5.01 us
    all_to_all x1, starting transfers between devices, on_device(): lax.all_to_all(send, 'lon', split_axis=0, concat_axis=0, tiled=True)  4.15 us
    pallas_call x1, Pallas kernels, pack(): pl.pallas_call(pack_kernel, out_shape=(jax.ShapeDtypeStruct((lon_count *...  3.29 us
  transfers between devices with their start and end apart: 6, of which 4 were waited for; matrix products, arithmetic and copies ran while one was open for 3% of the time, Pallas kernels for 0%

profile of v1, /device:TPU:12, one launch (start us, length us, event | category | flops | bytes accessed | tf_op | source)
XLA Modules:
  0.0 129.1 jit_solution(13376957885365174937)
XLA Ops:
  0.6 3.3 %pack.1 = (bf16[128,64,128]{2,1,0:T(8,128)(2,1)}, s32[64]{0:T(128)}, s32[256]{0:T(256)}) custom-call(s32[2,32]{1,0:T(2,128)} %bitcast.19, s32[2,32]{1,0:T(2,128)} %bitcast.20, s32[2,32]{1,0:T(2,128)} %bitcast.21, s32[2,32]{1,0:T(2,128)} %bitcast.22, bf16[64,64,128]{2,1,0:T(8,128)(2,1)} %bitcast.14), custom_call_target="tpu_custom_call" | custom-call | tf_op jit(solution)/shard_map/pack/pallas_call | solution.py:69
  3.9 0.7 slice.23
  4.6 0.1 all_to_all.13
  4.7 27.1 %all_to_all.21 = s32[32,4,1]{1,2,0:T(1,128)} all-to-all(s32[32,4,1]{1,2,0:T(1,128)S(1)} %bitcast.18), channel_id=1, replica_groups=mesh['lon'=32,'lat'=16] {'lon'}, dimensions={0} | all-to-all | bytes 1024 | tf_op jit(solution)/shard_map/all_to_all | solution.py:289
  31.8 0.0 copy-start
  31.8 0.0 copy-start.2
  31.8 0.0 copy-start.4
  31.8 0.0 copy-start.8
  31.8 4.2 %all-to-all-start.1 = ((bf16[128,64,128]{2,1,0:T(8,128)(2,1)}), bf16[128,64,128]{2,1,0:T(8,128)(2,1)S(1)}, u32[]{:S(2)}, u32[]{:S(2)}) async-start(bf16[128,64,128]{2,1,0:T(8,128)(2,1)} %get-tuple-element.15), calls=%async_computation.1 | async-start | bytes 4194304 | tf_op jit(solution)/shard_map/all_to_all | solution.py:286
  36.0 1.4 %slice_bitcast_fusion = (bf16[2,64,128]{2,1,0:T(8,128)(2,1)}, bf16[2,64,128]{2,1,0:T(8,128)(2,1)}) fusion(bf16[32,2,64,128]{3,2,1,0:T(8,128)(2,1)} %param.10), kind=kLoop, calls=%fused_computation | loop fusion | bytes 131072 | tf_op jit(solution)/shard_map/slice | solution.py:288
  37.4 3.0 %collective-permute-start = (bf16[2,64,128]{2,1,0:T(8,128)(2,1)}, bf16[2,64,128]{2,1,0:T(8,128)(2,1)}, u32[]{:S(2)}, u32[]{:S(2)}) collective-permute-start(bf16[2,64,128]{2,1,0:T(8,128)(2,1)} %get-tuple-element.25), channel_id=1, source_target_pairs={{0,1},{1,2},{2,3},{3,4},{4,5},{5,6},{6,7},{7,8},{8,9},{9,10},{10,1... | collective-permute-start | bytes 98312 | tf_op jit(solution)/shard_map/ppermute | solution.py:287
  40.4 2.8 %collective-permute-start.1 = (bf16[2,64,128]{2,1,0:T(8,128)(2,1)}, bf16[2,64,128]{2,1,0:T(8,128)(2,1)}, u32[]{:S(2)}, u32[]{:S(2)}) collective-permute-start(bf16[2,64,128]{2,1,0:T(8,128)(2,1)} %get-tuple-element.24), channel_id=1, source_target_pairs={{1,0},{2,1},{3,2},{4,3},{5,4},{6,5},{7,6},{8,7},{9,8},{10,9},{11,1... | collective-permute-start | bytes 98312 | tf_op jit(solution)/shard_map/ppermute | solution.py:288
  43.3 0.6 broadcast.3
  43.8 2.0 %reduce.3 = s32[32,4]{1,0:T(8,128)} reduce(s32[32,4,1]{1,2,0:T(1,128)} %all_to_all.21, s32[]{:T(128)} %broadcast.3), dimensions={2}, to_apply=%all_to_all.14.reduce_sub_computation.3 | reduce | bytes 1028 | tf_op jit(solution)/shard_map/all_to_all | solution.py:289
  45.9 0.8 all_to_all.15.codes
  46.7 0.0 collective-permute-done.before
  46.7 0.0 collective-permute-done.1.after
  46.7 47.0 %all-to-all-done.1.received = bf16[128,64,128]{2,1,0:T(8,128)(2,1)S(1)} async-done(((bf16[128,64,128]{2,1,0:T(8,128)(2,1)}), bf16[128,64,128]{2,1,0:T(8,128)(2,1)S(1)}, u32[]{:S(2)}, u32[]{:S(2)}) %all-to-all-start.1) | async-done | bytes 2097184 | tf_op jit(solution)/shard_map/all_to_all | solution.py:286
  93.7 0.0 copy-done
  93.7 0.0 copy-done.2
  93.7 0.0 copy-done.3
  93.7 0.0 copy-done.4
  93.7 0.0 copy-done.8
  93.8 0.0 copy-start.1
  93.8 1.2 copy-done.1
  95.0 6.9 %adjoint.1 = (bf16[64,64,128]{2,1,0:T(8,128)(2,1)}, f32[4,64,128]{2,1,0:T(8,128)S(1)}, bf16[2,64,128]{2,1,0:T(8,128)(2,1)S(1)}, bf16[2,64,128]{2,1,0:T(8,128)(2,...) custom-call(s32[64]{0:T(128)S(1)} %copy-done.8, s32[128]{0:T(128)S(1)} %all_to_all.15.codes, ...), custom_call_target="tpu_custom_call" | custom-call | tf_op jit(solution)/shard_map/adjoint/pallas_call | solution.py:197
  101.9 0.0 copy-start.5
  101.9 0.6 copy-done.5
  102.5 0.0 copy-start.6
  102.5 0.6 copy-done.6
  103.2 0.0 copy-start.7
  103.2 0.6 copy-done.7
  103.8 0.0 copy-start.9
  103.8 0.6 copy-done.9
  104.4 0.0 copy-start.10
  104.4 0.6 copy-done.10
  105.0 7.1 %all-to-all-start.2 = ((f32[128,2,128]{2,1,0:T(2,128)}), f32[128,2,128]{2,1,0:T(2,128)S(1)}, u32[]{:S(2)}, u32[]{:S(2)}) async-start(f32[128,2,128]{2,1,0:T(2,128)} %copy-done.5), calls=%async_computation.2 | async-start | bytes 262144 | tf_op jit(solution)/shard_map/all_to_all | solution.py:293
  112.1 2.9 %collective-permute-start.2 = (bf16[2,64,128]{2,1,0:T(8,128)(2,1)}, bf16[2,64,128]{2,1,0:T(8,128)(2,1)S(1)}, u32[]{:S(2)}, u32[]{:S(2)}) collective-permute-start(bf16[2,64,128]{2,1,0:T(8,128)(2,1)} %copy-done.10), channel_id=1, source_target_pairs={{0,1},{1,2},{2,3},{3,4},{4,5},{5,6},{6,7},{7,8},{8,9},{9,10},{10,1... | collective-permute-start | bytes 98312 | tf_op jit(solution)/shard_map/ppermute | solution.py:295
  115.1 2.9 %collective-permute-start.3 = (bf16[2,64,128]{2,1,0:T(8,128)(2,1)}, bf16[2,64,128]{2,1,0:T(8,128)(2,1)S(1)}, u32[]{:S(2)}, u32[]{:S(2)}) collective-permute-start(bf16[2,64,128]{2,1,0:T(8,128)(2,1)} %copy-done.9), channel_id=1, source_target_pairs={{1,0},{2,1},{3,2},{4,3},{5,4},{6,5},{7,6},{8,7},{9,8},{10,9},{11,1... | collective-permute-start | bytes 98312 | tf_op jit(solution)/shard_map/ppermute | solution.py:294
  118.0 0.2 collective-permute-done.2.from_before
  118.2 0.0 copy-start.12
  118.2 2.9 %collective-permute-done.3.from_after = bf16[2,64,128]{2,1,0:T(8,128)(2,1)S(1)} collective-permute-done((bf16[2,64,128]{2,1,0:T(8,128)(2,1)}, bf16[2,64,128]{2,1,0:T(8,128)(2,1)S(1)}, u32[]{:S(2)}, u32[]{:S(2)}) %collective-permute-start.3) | collective-permute-done | bytes 32800 | tf_op jit(solution)/shard_map/ppermute | solution.py:294
  121.1 0.0 copy-start.13
  121.1 5.0 %all-to-all-done.2.returned = f32[128,2,128]{2,1,0:T(2,128)S(1)} async-done(((f32[128,2,128]{2,1,0:T(2,128)}), f32[128,2,128]{2,1,0:T(2,128)S(1)}, u32[]{:S(2)}, u32[]{:S(2)}) %all-to-all-start.2) | async-done | bytes 131104 | tf_op jit(solution)/shard_map/all_to_all | solution.py:293
  126.1 0.0 copy-done.12
  126.1 0.0 copy-done.13
  126.1 0.6 copy-done.11
  126.7 2.3 %finish.1 = (bf16[64,64,128]{2,1,0:T(8,128)(2,1)}, f32[64,2,128]{2,1,0:T(2,128)}) custom-call(s32[64]{0:T(128)} %get-tuple-element.13.places, f32[128,2,128]{2,1,0:T(2,128)} %copy-done.11, f32[64,2,128]{2,1,0:T(2,128)} %copy-done.7, f32[4,64,128]{2,1,0:T(8,128)} %copy-done.6, bf16[2,64,128]{2,1,0:T(8,128)(2,1)} %copy-done.12, ...), custom_call_target="tpu_custom_call", output_to_operand_aliasing={{0}: (6, {})} | custom-call | tf_op jit(solution)/shard_map/finish/pallas_call | solution.py:255
  (2 shorter events, 0.0 us)
Async XLA Ops:
  31.8 61.9 %copy-start = (bf16[32,2,64,128]{3,2,1,0:T(8,128)(2,1)S(1)}, bf16[32,2,64,128]{3,2,1,0:T(8,128)(2,1)}, u32[]{:S(2)}) copy-start(bf16[32,2,64,128]{3,2,1,0:T(8,128)(2,1)} %param.9) | copy-start | bytes 3145732
  31.8 61.9 %copy-start.2 = (bf16[4,128,128]{2,1,0:T(8,128)(2,1)S(1)}, bf16[4,128,128]{2,1,0:T(8,128)(2,1)}, u32[]{:S(2)}) copy-start(bf16[4,128,128]{2,1,0:T(8,128)(2,1)} %blend.1) | copy-start | bytes 393220
  31.8 61.9 %copy-start.3 = (bf16[4,128,128]{2,1,0:T(8,128)(2,1)S(1)}, bf16[4,128,128]{2,1,0:T(8,128)(2,1)}, u32[]{:S(2)}) copy-start(bf16[4,128,128]{2,1,0:T(8,128)(2,1)} %east.1) | copy-start | bytes 393220
  31.8 61.9 %copy-start.4 = (bf16[4,128,128]{2,1,0:T(8,128)(2,1)S(1)}, bf16[4,128,128]{2,1,0:T(8,128)(2,1)}, u32[]{:S(2)}) copy-start(bf16[4,128,128]{2,1,0:T(8,128)(2,1)} %north.1) | copy-start | bytes 393220
  31.8 61.9 %copy-start.8 = (s32[64]{0:T(128)S(1)}, s32[64]{0:T(128)}, u32[]{:S(2)}) copy-start(s32[64]{0:T(128)} %get-tuple-element.13.places) | copy-start | bytes 772
  31.8 61.9 %all-to-all-start.1 = ((bf16[128,64,128]{2,1,0:T(8,128)(2,1)}), bf16[128,64,128]{2,1,0:T(8,128)(2,1)S(1)}, u32[]{:S(2)}, u32[]{:S(2)}) async-start(bf16[128,64,128]{2,1,0:T(8,128)(2,1)} %get-tuple-element.15), calls=%async_computation.1 | async-start | bytes 4194304 | tf_op jit(solution)/shard_map/all_to_all | solution.py:286
  37.4 9.3 %collective-permute-start = (bf16[2,64,128]{2,1,0:T(8,128)(2,1)}, bf16[2,64,128]{2,1,0:T(8,128)(2,1)}, u32[]{:S(2)}, u32[]{:S(2)}) collective-permute-start(bf16[2,64,128]{2,1,0:T(8,128)(2,1)} %get-tuple-element.25), channel_id=1, source_target_pairs={{0,1},{1,2},{2,3},{3,4},{4,5},{5,6},{6,7},{7,8},{8,9},{9,10},{10,1... | collective-permute-start | bytes 98312 | tf_op jit(solution)/shard_map/ppermute | solution.py:287
  40.4 6.3 %collective-permute-start.1 = (bf16[2,64,128]{2,1,0:T(8,128)(2,1)}, bf16[2,64,128]{2,1,0:T(8,128)(2,1)}, u32[]{:S(2)}, u32[]{:S(2)}) collective-permute-start(bf16[2,64,128]{2,1,0:T(8,128)(2,1)} %get-tuple-element.24), channel_id=1, source_target_pairs={{1,0},{2,1},{3,2},{4,3},{5,4},{6,5},{7,6},{8,7},{9,8},{10,9},{11,1... | collective-permute-start | bytes 98312 | tf_op jit(solution)/shard_map/ppermute | solution.py:288
  93.8 1.2 copy-start.1
  101.9 0.7 copy-start.5
  102.5 0.7 copy-start.6
  103.2 0.6 copy-start.7
  103.8 0.6 copy-start.9
  104.4 0.6 copy-start.10
  105.0 21.1 %all-to-all-start.2 = ((f32[128,2,128]{2,1,0:T(2,128)}), f32[128,2,128]{2,1,0:T(2,128)S(1)}, u32[]{:S(2)}, u32[]{:S(2)}) async-start(f32[128,2,128]{2,1,0:T(2,128)} %copy-done.5), calls=%async_computation.2 | async-start | bytes 262144 | tf_op jit(solution)/shard_map/all_to_all | solution.py:293
  112.1 6.0 %collective-permute-start.2 = (bf16[2,64,128]{2,1,0:T(8,128)(2,1)}, bf16[2,64,128]{2,1,0:T(8,128)(2,1)S(1)}, u32[]{:S(2)}, u32[]{:S(2)}) collective-permute-start(bf16[2,64,128]{2,1,0:T(8,128)(2,1)} %copy-done.10), channel_id=1, source_target_pairs={{0,1},{1,2},{2,3},{3,4},{4,5},{5,6},{6,7},{7,8},{8,9},{9,10},{10,1... | collective-permute-start | bytes 98312 | tf_op jit(solution)/shard_map/ppermute | solution.py:295
  115.1 6.0 %collective-permute-start.3 = (bf16[2,64,128]{2,1,0:T(8,128)(2,1)}, bf16[2,64,128]{2,1,0:T(8,128)(2,1)S(1)}, u32[]{:S(2)}, u32[]{:S(2)}) collective-permute-start(bf16[2,64,128]{2,1,0:T(8,128)(2,1)} %copy-done.9), channel_id=1, source_target_pairs={{1,0},{2,1},{3,2},{4,3},{5,4},{6,5},{7,6},{8,7},{9,8},{10,9},{11,1... | collective-permute-start | bytes 98312 | tf_op jit(solution)/shard_map/ppermute | solution.py:294
  118.2 7.9 %copy-start.12 = (bf16[2,64,128]{2,1,0:T(8,128)(2,1)}, bf16[2,64,128]{2,1,0:T(8,128)(2,1)S(1)}, u32[]{:S(2)}) copy-start(bf16[2,64,128]{2,1,0:T(8,128)(2,1)S(1)} %collective-permute-done.2.from_before) | copy-start | bytes 98308
  121.1 5.0 %copy-start.13 = (bf16[2,64,128]{2,1,0:T(8,128)(2,1)}, bf16[2,64,128]{2,1,0:T(8,128)(2,1)S(1)}, u32[]{:S(2)}) copy-start(bf16[2,64,128]{2,1,0:T(8,128)(2,1)S(1)} %collective-permute-done.3.from_after) | copy-start | bytes 98308
  126.1 0.7 copy-start.11

commit v2 on v1

v2 whole, which is shorter than its diff:
```python
import functools

import jax
import jax.numpy as jnp
from jax import lax
from jax.experimental import pallas as pl
from jax.experimental.pallas import tpu as pltpu
from jax.sharding import PartitionSpec as P

CAP = 4
META = 16
KINDS = 4
CODES = 512
EXACT = 200
UNROLL = 8
PARTS = 4
VMEM_LIMIT = 24 * 1024 * 1024


def in_hbm(array):
    return pltpu.with_memory_space_constraint(array, pltpu.HBM)


def in_vmem(array):
    return pltpu.with_memory_space_constraint(array, pltpu.VMEM)


def pack_kernel(owner, step, column, kind, adjoint, send, places, codes, counts, tiles, meta, load_sem, sem, meta_sem):
    tile_cols, tile_rows = owner.shape
    tiles_here, levels, _ = adjoint.shape
    lon_count = counts.shape[0]
    me = lax.axis_index("lon")
    load = pltpu.make_async_copy(adjoint, tiles, load_sem)
    load.start()

    for d in range(lon_count):
        counts[d] = 0
        for r in range(CAP):
            codes[d * CAP + r] = 0

    def place_rows(n, sent):
        for u in range(4):
            i = n * 4 + u
            for j in range(tile_cols):
                to = owner[j, i]
                rank = counts[to]
                remote = to != me
                counts[to] = rank + 1
                block = (i + step[j, i]) * tile_cols + column[j, i]
                code = block * KINDS + kind[j, i] + 1
                places[i * tile_cols + j] = jnp.where(remote, to * CAP + rank, -code)
                codes[jnp.where(remote, to * CAP + rank, me * CAP)] = jnp.where(remote, code, 0)
                sent = sent + remote.astype(jnp.int32)
        return sent

    sent = lax.fori_loop(0, tile_rows // 4, place_rows, 0)
    load.wait()

    def send_rows(n, carry):
        for u in range(8):
            tile = n * 8 + u
            slot = places[tile]

            @pl.when(slot >= 0)
            def _():
                rows = pl.ds(pl.multiple_of((slot & (CAP - 1)) * levels, levels), levels)
                pltpu.make_async_copy(tiles.at[tile], send.at[slot // CAP, rows, :], sem).start()

        return carry

    lax.fori_loop(0, tiles_here // 8, send_rows, 0)
    lane = lax.broadcasted_iota(jnp.int32, (META, 128), 1)

    def describe(n, carry):
        for u in range(4):
            d = n * 4 + u
            line = jnp.zeros((META, 128), jnp.int32)
            for r in range(CAP):
                code = codes[d * CAP + r]
                line = jnp.where(lane == r, jnp.where(code > EXACT, EXACT - code, code), line)
            meta[d] = line.astype(jnp.float32).astype(jnp.bfloat16)
        return carry

    lax.fori_loop(0, lon_count // 4, describe, 0)
    told = pltpu.make_async_copy(meta, send.at[:, pl.ds(CAP * levels, META), :], meta_sem)
    told.start()

    def settle(_, carry):
        pltpu.make_async_copy(tiles.at[0], send.at[0, pl.ds(0, levels), :], sem).wait()
        return carry

    lax.fori_loop(0, sent, settle, 0)
    told.wait()


def pack(owner, step, column, kind, adjoint, lon_count):
    tiles_here, levels, width = adjoint.shape
    smem = pl.BlockSpec(memory_space=pltpu.SMEM)
    hbm = pl.BlockSpec(memory_space=pltpu.HBM)
    return pl.pallas_call(
        pack_kernel,
        out_shape=(
            pltpu.HBM((lon_count, CAP * levels + META, width), jnp.bfloat16),
            jax.ShapeDtypeStruct((tiles_here,), jnp.int32),
        ),
        in_specs=[smem, smem, smem, smem, hbm],
        out_specs=(hbm, smem),
        scratch_shapes=[
            pltpu.SMEM((lon_count * CAP,), jnp.int32),
            pltpu.SMEM((lon_count,), jnp.int32),
            pltpu.VMEM((tiles_here, levels, width), jnp.bfloat16),
            pltpu.VMEM((lon_count, META, width), jnp.bfloat16),
            pltpu.SemaphoreType.DMA,
            pltpu.SemaphoreType.DMA,
            pltpu.SemaphoreType.DMA,
        ],
        compiler_params=pltpu.CompilerParams(vmem_limit_bytes=60 * 1024 * 1024),
        name="pack",
    )(owner, step, column, kind, in_hbm(adjoint))


def adjoint_kernel(
    places, received, adjoint, old, before, after, blend, east, north,
    result, edge_own, cross_before, cross_after, sensed_remote, sensed_home,
    tiles, sources, sums, remote, home, rounded, edges, back, slopes, listed, codes, work, counts,
    sem, code_sem, out_sem,
):
    lon_count = received.shape[0]
    tiles_here, levels, width = adjoint.shape
    slot_count = lon_count * CAP
    tile_cols = before.shape[0]
    block_count = tiles_here + 2 * tile_cols
    room = work.shape[0] // (2 * KINDS)
    me = lax.axis_index("lon")

    line = received[:, CAP * levels : CAP * levels + META, :].astype(jnp.float32)[:, 0, :].astype(jnp.int32)
    listed[...] = jnp.where(line < 0, EXACT - line, line)
    code_copy = pltpu.make_async_copy(listed, codes, code_sem)
    code_copy.start()
    loads = [
        pltpu.make_async_copy(old, sources.at[pl.ds(tile_cols, tiles_here)], sem.at[0]),
        pltpu.make_async_copy(before, sources.at[pl.ds(0, tile_cols)], sem.at[1]),
        pltpu.make_async_copy(after, sources.at[pl.ds(tile_cols + tiles_here, tile_cols)], sem.at[2]),
        pltpu.make_async_copy(adjoint, tiles, sem.at[3]),
    ]
    for copy in loads:
        copy.start()
    for k in range(KINDS):
        back[k] = blend[k].T
        slopes[k, :, :width] = east[k]
        slopes[k, :, width:] = north[k]

    def clear(b, carry):
        sums[b] = jnp.zeros((levels, width), jnp.float32)
        return carry

    lax.fori_loop(0, block_count + 1, clear, 0, unroll=3)

    for k in range(2 * KINDS):
        counts[k] = 0

    def enlist(where, entry, code, valid):
        row = where * KINDS + (code & (KINDS - 1))
        n = counts[row]
        work[row * room + n] = entry * CODES + code
        counts[row] = n + valid.astype(jnp.int32)

    def enlist_home(n, carry):
        for u in range(8):
            place = places[n * 8 + u]
            enlist(1, n * 8 + u, -place - 1, place < 0)
        return carry

    lax.fori_loop(0, tiles_here // 8, enlist_home, 0)
    code_copy.wait()

    def enlist_remote(n, carry):
        for u in range(2):
            s = n * 2 + u
            for r in range(CAP):
                code = codes[s, r]
                enlist(0, s * CAP + r, code - 1, (code > 0) & (s != me))
        return carry

    lax.fori_loop(0, lon_count // 2, enlist_remote, 0)
    for k in range(KINDS):
        for where, spare in ((0, slot_count), (1, tiles_here)):
            row = where * KINDS + k
            n = counts[row]
            for u in range(UNROLL):
                work[row * room + n + u] = spare * CODES + block_count * KINDS + k
    for copy in loads:
        copy.wait()

    def arrived_tile(p):
        p = jnp.minimum(p, slot_count - 1)
        rows = pl.ds(pl.multiple_of((p & (CAP - 1)) * levels, levels), levels)
        return received[p // CAP, rows, :]

    def home_tile(p):
        return tiles[jnp.minimum(p, tiles_here - 1)]

    def some_tiles(row, kind, tile_at, sensed, n):
        entries = [work[row * room + n * UNROLL + u] for u in range(UNROLL)]
        place = [e // CODES for e in entries]
        block = [(e & (CODES - 1)) // KINDS for e in entries]
        arrived = [tile_at(p) for p in place]
        source = [sources[jnp.minimum(b, block_count - 1)] for b in block]
        spread = jnp.dot(jnp.concatenate(arrived, axis=0), back[kind], preferred_element_type=jnp.float32)
        slope = jnp.dot(jnp.concatenate(source, axis=0), slopes[kind], preferred_element_type=jnp.float32)
        for u in range(UNROLL):
            full = arrived[u].astype(jnp.float32)
            s = slope[u * levels : (u + 1) * levels]
            sensed[place[u], 0:1] = jnp.sum(full * s[:, :width], axis=0, keepdims=True)
            sensed[place[u], 1:2] = jnp.sum(full * s[:, width:], axis=0, keepdims=True)
        for u in range(UNROLL):
            s = spread[u * levels : (u + 1) * levels]
            sums[block[u]] += s.astype(jnp.bfloat16).astype(jnp.float32)

    for where, tile_at, sensed in ((0, arrived_tile, remote), (1, home_tile, home)):
        for kind in range(KINDS):
            row = where * KINDS + kind

            def step(n, carry, row=row, kind=kind, tile_at=tile_at, sensed=sensed):
                some_tiles(row, kind, tile_at, sensed, n)
                return carry

            lax.fori_loop(0, (counts[row] + UNROLL - 1) // UNROLL, step, 0)

    copies = []

    def put(source, target):
        copy = pltpu.make_async_copy(source, target, out_sem.at[len(copies)])
        copy.start()
        copies.append(copy)

    put(remote.at[pl.ds(0, slot_count)], sensed_remote)
    put(home.at[pl.ds(0, tiles_here)], sensed_home)
    for c in range(tile_cols):
        edges[c] = sums[c].astype(jnp.bfloat16)
        edges[tile_cols + c] = sums[tile_cols + tiles_here + c].astype(jnp.bfloat16)
    put(edges.at[pl.ds(0, tile_cols)], cross_before)
    put(edges.at[pl.ds(tile_cols, tile_cols)], cross_after)
    put(sums.at[pl.ds(tile_cols, tile_cols)], edge_own.at[pl.ds(0, tile_cols)])
    put(sums.at[pl.ds(tiles_here, tile_cols)], edge_own.at[pl.ds(tile_cols, tile_cols)])

    def finish(b, carry):
        rounded[b] = sums[tile_cols + b].astype(jnp.bfloat16)
        return carry

    part = tiles_here // PARTS
    for p in range(PARTS):
        lax.fori_loop(p * part, (p + 1) * part, finish, 0, unroll=4)
        put(rounded.at[pl.ds(p * part, part)], result.at[pl.ds(p * part, part)])
    for copy in copies:
        copy.wait()


def adjoint_step(places, received, adjoint, old, before, after, blend, east, north):
    lon_count = received.shape[0]
    slot_count = lon_count * CAP
    tiles_here, levels, width = adjoint.shape
    tile_cols = before.shape[0]
    block_count = tiles_here + 2 * tile_cols
    assert (block_count + 1) * KINDS <= CODES and block_count * KINDS <= EXACT + 256
    smem = pl.BlockSpec(memory_space=pltpu.SMEM)
    vmem = pl.BlockSpec(memory_space=pltpu.VMEM)
    hbm = pl.BlockSpec(memory_space=pltpu.HBM)
    edge = pltpu.HBM((tile_cols, levels, width), jnp.bfloat16)
    return pl.pallas_call(
        adjoint_kernel,
        out_shape=(
            pltpu.HBM((tiles_here, levels, width), jnp.bfloat16),
            pltpu.HBM((2 * tile_cols, levels, width), jnp.float32),
            edge,
            edge,
            pltpu.HBM((slot_count, 2, width), jnp.float32),
            pltpu.HBM((tiles_here, 2, width), jnp.float32),
        ),
        in_specs=[smem, vmem, hbm, hbm, hbm, hbm, vmem, vmem, vmem],
        out_specs=(hbm,) * 6,
        scratch_shapes=[
            pltpu.VMEM((tiles_here, levels, width), jnp.bfloat16),
            pltpu.VMEM((block_count, levels, width), jnp.bfloat16),
            pltpu.VMEM((block_count + 1, levels, width), jnp.float32),
            pltpu.VMEM((slot_count + 1, 2, width), jnp.float32),
            pltpu.VMEM((tiles_here + 1, 2, width), jnp.float32),
            pltpu.VMEM((tiles_here, levels, width), jnp.bfloat16),
            pltpu.VMEM((2 * tile_cols, levels, width), jnp.bfloat16),
            pltpu.VMEM((KINDS, width, width), jnp.bfloat16),
            pltpu.VMEM((KINDS, width, 2 * width), jnp.bfloat16),
            pltpu.VMEM((lon_count, width), jnp.int32),
            pltpu.SMEM((lon_count, width), jnp.int32),
            pltpu.SMEM((2 * KINDS * (slot_count + UNROLL),), jnp.int32),
            pltpu.SMEM((2 * KINDS,), jnp.int32),
            pltpu.SemaphoreType.DMA((4,)),
            pltpu.SemaphoreType.DMA,
            pltpu.SemaphoreType.DMA((6 + PARTS,)),
        ],
        compiler_params=pltpu.CompilerParams(vmem_limit_bytes=VMEM_LIMIT),
        name="adjoint",
    )(places, in_vmem(received), in_hbm(adjoint), in_hbm(old), in_hbm(before), in_hbm(after), blend, east, north)


def finish_kernel(places, returned, sensed_home, edge_own, from_before, from_after, _, result, sensed, edges, out, sem):
    tiles_here = sensed.shape[0]
    tile_cols = from_before.shape[0]
    for c in range(tile_cols):
        edges[c] = (edge_own[c] + from_before[c].astype(jnp.float32)).astype(jnp.bfloat16)
        edges[tile_cols + c] = (edge_own[tile_cols + c] + from_after[c].astype(jnp.float32)).astype(jnp.bfloat16)
    copies = [
        pltpu.make_async_copy(edges.at[pl.ds(0, tile_cols)], result.at[pl.ds(0, tile_cols)], sem.at[0]),
        pltpu.make_async_copy(
            edges.at[pl.ds(tile_cols, tile_cols)],
            result.at[pl.ds(tiles_here - tile_cols, tile_cols)],
            sem.at[1],
        ),
        pltpu.make_async_copy(out, sensed, sem.at[2]),
    ]
    copies[0].start()
    copies[1].start()

    def place_some(n, carry):
        for u in range(8):
            t = n * 8 + u
            place = places[t]
            out[t] = jnp.where(place < 0, sensed_home[t], returned[jnp.maximum(place, 0)])
        return carry

    lax.fori_loop(0, tiles_here // 8, place_some, 0)
    copies[2].start()
    for copy in copies:
        copy.wait()


def finish(places, returned, sensed_home, edge_own, from_before, from_after, partial):
    tiles_here, _, width = sensed_home.shape
    smem = pl.BlockSpec(memory_space=pltpu.SMEM)
    vmem = pl.BlockSpec(memory_space=pltpu.VMEM)
    hbm = pl.BlockSpec(memory_space=pltpu.HBM)
    return pl.pallas_call(
        finish_kernel,
        out_shape=(
            jax.ShapeDtypeStruct(partial.shape, partial.dtype),
            jax.ShapeDtypeStruct((tiles_here, 2, width), jnp.float32),
        ),
        in_specs=[smem] + [vmem] * 5 + [hbm],
        out_specs=(hbm, hbm),
        scratch_shapes=[
            pltpu.VMEM(edge_own.shape, jnp.bfloat16),
            pltpu.VMEM((tiles_here, 2, width), jnp.float32),
            pltpu.SemaphoreType.DMA((3,)),
        ],
        input_output_aliases={6: 0},
        compiler_params=pltpu.CompilerParams(vmem_limit_bytes=8 * 1024 * 1024),
        name="finish",
    )(places, returned, sensed_home, edge_own, from_before, from_after, partial)


def on_device(
    tracer_adjoint, tracer_old, owner_lon, row_step, owner_column, tile_kind, blend_weights, slope_east, slope_north
):
    lon_count = lax.axis_size("lon")
    lat_count = lax.axis_size("lat")
    tile_rows, tile_cols = owner_lon.shape
    levels, width = tracer_adjoint.shape[2:]
    tiles_here = tile_rows * tile_cols
    north_to_south = [(i, i + 1) for i in range(lat_count - 1)]
    south_to_north = [(j, i) for i, j in north_to_south]
    adjoint = tracer_adjoint.reshape(tiles_here, levels, width)
    old = tracer_old.reshape(tiles_here, levels, width)

    send, places = pack(owner_lon.T, row_step.T, owner_column.T, tile_kind.T, adjoint, lon_count)
    received = lax.all_to_all(send, "lon", split_axis=0, concat_axis=0, tiled=True)
    before = lax.ppermute(old[-tile_cols:], "lat", north_to_south)
    after = lax.ppermute(old[:tile_cols], "lat", south_to_north)
    partial, edge_own, cross_before, cross_after, sensed_remote, sensed_home = adjoint_step(
        places, received, adjoint, old, before, after, blend_weights, slope_east, slope_north
    )
    returned = lax.all_to_all(sensed_remote, "lon", split_axis=0, concat_axis=0, tiled=True)
    from_after = lax.ppermute(cross_before, "lat", south_to_north)
    from_before = lax.ppermute(cross_after, "lat", north_to_south)
    result, sensed = finish(places, returned, sensed_home, edge_own, from_before, from_after, partial)
    return (
        result.reshape(tracer_old.shape),
        sensed.reshape(tile_rows, tile_cols, 2, width),
    )


def solution(mesh):
    return jax.shard_map(
        on_device,
        mesh=mesh,
        in_specs=(
            P("lat", "lon", None, None),
            P("lat", "lon", None, None),
            P("lat", "lon"),
            P("lat", "lon"),
            P("lat", "lon"),
            P("lat", "lon"),
            P(),
            P(),
            P(),
        ),
        out_specs=(P("lat", "lon", None, None), P("lat", "lon", None, None)),
        check_vma=False,
    )
```

time: 130 us -> 112 us (0.86)
  the two profiles are of different devices: /device:TPU:12 before, /device:TPU:8 now
where the time goes in v2:
time: 112 us; the launch traced here: 111 us
  waiting for transfers between devices  57.8 us (52%)
  starting transfers between devices  37.4 us (33%)
  Pallas kernels  12.4 us (11%)
  local copies, waits for them, and re-layouts  2.56 us (2%)
    ppermute x1, waiting for transfers between devices, on_device(): before = lax.ppermute(old[-tile_cols:], 'lat', north_to_south)  46.5 us
    all_to_all x1, starting transfers between devices, on_device(): lax.all_to_all(send, 'lon', split_axis=0, concat_axis=0, tiled=True)  15.2 us
    pallas_call x1, Pallas kernels, adjoint_step(): pl.pallas_call(adjoint_kernel, out_shape=(pltpu.HBM((tiles_here, levels,...  7.29 us
    all_to_all x1, starting transfers between devices, on_device(): lax.all_to_all(sensed_remote, 'lon', split_axis=0, concat_axis=0, tiled=T...  6.32 us
    ppermute x1, starting transfers between devices, on_device(): from_after = lax.ppermute(cross_before, 'lat', south_to_north)  5.6 us
    all_to_all x1, waiting for transfers between devices, on_device(): lax.all_to_all(send, 'lon', split_axis=0, concat_axis=0, tiled=True)  5.36 us
    ppermute x1, starting transfers between devices, on_device(): after = lax.ppermute(old[:tile_cols], 'lat', south_to_north)  4.64 us
    all_to_all x1, waiting for transfers between devices, on_device(): lax.all_to_all(sensed_remote, 'lon', split_axis=0, concat_axis=0, tiled=T...  4.01 us
  transfers between devices with their start and end apart: 6, of which 5 were waited for; matrix products, arithmetic and copies ran while one was open for 1% of the time, Pallas kernels for 0%

profile of v2, /device:TPU:8, one launch (start us, length us, event | category | flops | bytes accessed | tf_op | source)
XLA Modules:
  0.0 111.0 jit_solution(5639600142719477282)
XLA Ops:
  0.6 3.7 %pack.1 = (bf16[32,272,128]{2,1,0:T(8,128)(2,1)}, s32[64]{0:T(128)}) custom-call(s32[2,32]{1,0:T(2,128)} %bitcast.16, s32[2,32]{1,0:T(2,128)} %bitcast.17, s32[2,32]{1,0:T(2,128)} %bitcast.18, s32[2,32]{1,0:T(2,128)} %bitcast.19, bf16[64,64,128]{2,1,0:T(8,128)(2,1)} %bitcast.12), custom_call_target="tpu_custom_call" | custom-call | tf_op jit(solution)/shard_map/pack/pallas_call | solution.py:100
  4.4 0.0 copy-start
  4.4 0.0 copy-start.1
  4.4 0.0 copy-start.2
  4.4 0.0 copy-start.5
  4.4 15.2 %all-to-all-start = ((bf16[32,272,128]{2,1,0:T(8,128)(2,1)}), bf16[32,272,128]{2,1,0:T(8,128)(2,1)S(1)}, u32[]{:S(2)}, u32[]{:S(2)}) async-start(bf16[32,272,128]{2,1,0:T(8,128)(2,1)} %get-tuple-element.13), calls=%async_computation | async-start | bytes 4456448 | tf_op jit(solution)/shard_map/all_to_all | solution.py:374
  19.7 0.8 slice_bitcast_fusion
  20.4 3.3 %collective-permute-start = (bf16[2,64,128]{2,1,0:T(8,128)(2,1)S(1)}, bf16[2,64,128]{2,1,0:T(8,128)(2,1)S(1)}, u32[]{:S(2)}, u32[]{:S(2)}) collective-permute-start(bf16[2,64,128]{2,1,0:T(8,128)(2,1)S(1)} %get-tuple-element.23), channel_id=1, source_target_pairs={{0,1},{1,2},{2,3},{3,4},{4,5},{5,6},{6,7},{7,8},{8,9},{9,10},{10,1... | collective-permute-start | bytes 98312 | tf_op jit(solution)/shard_map/ppermute | solution.py:375
  23.7 4.6 %collective-permute-start.1 = (bf16[2,64,128]{2,1,0:T(8,128)(2,1)S(1)}, bf16[2,64,128]{2,1,0:T(8,128)(2,1)S(1)}, u32[]{:S(2)}, u32[]{:S(2)}) collective-permute-start(bf16[2,64,128]{2,1,0:T(8,128)(2,1)S(1)} %get-tuple-element.22), channel_id=1, source_target_pairs={{1,0},{2,1},{3,2},{4,3},{5,4},{6,5},{7,6},{8,7},{9,8},{10,9},{11,1... | collective-permute-start | bytes 98312 | tf_op jit(solution)/shard_map/ppermute | solution.py:376
  28.4 46.5 %collective-permute-done.before = bf16[2,64,128]{2,1,0:T(8,128)(2,1)S(1)} collective-permute-done((bf16[2,64,128]{2,1,0:T(8,128)(2,1)S(1)}, bf16[2,64,128]{2,1,0:T(8,128)(2,1)S(1)}, u32[]{:S(2)}, u32[]{:S(2)}) %collective-permute-start) | collective-permute-done | bytes 32800 | tf_op jit(solution)/shard_map/ppermute | solution.py:375
  74.9 0.0 copy-start.6
  74.9 0.0 collective-permute-done.1.after
  74.9 0.0 copy-start.7
  74.9 5.4 %all-to-all-done.received = bf16[32,272,128]{2,1,0:T(8,128)(2,1)S(1)} async-done(((bf16[32,272,128]{2,1,0:T(8,128)(2,1)}), bf16[32,272,128]{2,1,0:T(8,128)(2,1)S(1)}, u32[]{:S(2)}, u32[]{:S(2)}) %all-to-all-start) | async-done | bytes 2228256 | tf_op jit(solution)/shard_map/all_to_all | solution.py:374
  80.3 0.0 copy-done.6
  80.3 0.0 copy-done.7
  80.3 0.0 copy-done
  80.3 0.0 copy-done.1
  80.3 0.0 copy-done.2
  80.3 0.0 copy-done.5
  80.3 7.3 %adjoint.1 = (bf16[64,64,128]{2,1,0:T(8,128)(2,1)}, f32[4,64,128]{2,1,0:T(8,128)}, bf16[2,64,128]{2,1,0:T(8,128)(2,1)}, bf16[2,64,128]{2,1,0:T(8,128)(2,1)}, f32...) custom-call(s32[64]{0:T(128)S(1)} %copy-done.5, bf16[32,272,128]{2,1,0:T(8,128)(2,1)S(1)} %all-to-all-done.received, ...), custom_call_target="tpu_custom_call" | custom-call | tf_op jit(solution)/shard_map/adjoint/pallas_call | solution.py:270
  87.6 6.3 %all-to-all-start.1 = ((f32[128,2,128]{2,1,0:T(2,128)}), f32[128,2,128]{2,1,0:T(2,128)S(1)}, u32[]{:S(2)}, u32[]{:S(2)}) async-start(f32[128,2,128]{2,1,0:T(2,128)} %get-tuple-element.14), calls=%async_computation.1 | async-start | bytes 262144 | tf_op jit(solution)/shard_map/all_to_all | solution.py:380
  94.0 2.4 %collective-permute-start.2 = (bf16[2,64,128]{2,1,0:T(8,128)(2,1)}, bf16[2,64,128]{2,1,0:T(8,128)(2,1)S(1)}, u32[]{:S(2)}, u32[]{:S(2)}) collective-permute-start(bf16[2,64,128]{2,1,0:T(8,128)(2,1)} %get-tuple-element.17), channel_id=1, source_target_pairs={{0,1},{1,2},{2,3},{3,4},{4,5},{5,6},{6,7},{7,8},{8,9},{9,10},{10,1... | collective-permute-start | bytes 98312 | tf_op jit(solution)/shard_map/ppermute | solution.py:382
  96.3 5.6 %collective-permute-start.3 = (bf16[2,64,128]{2,1,0:T(8,128)(2,1)}, bf16[2,64,128]{2,1,0:T(8,128)(2,1)S(1)}, u32[]{:S(2)}, u32[]{:S(2)}) collective-permute-start(bf16[2,64,128]{2,1,0:T(8,128)(2,1)} %get-tuple-element.18), channel_id=1, source_target_pairs={{1,0},{2,1},{3,2},{4,3},{5,4},{6,5},{7,6},{8,7},{9,8},{10,9},{11,1... | collective-permute-start | bytes 98312 | tf_op jit(solution)/shard_map/ppermute | solution.py:381
  101.9 0.3 collective-permute-done.2.from_before
  102.3 1.6 %collective-permute-done.3.from_after = bf16[2,64,128]{2,1,0:T(8,128)(2,1)S(1)} collective-permute-done((bf16[2,64,128]{2,1,0:T(8,128)(2,1)}, bf16[2,64,128]{2,1,0:T(8,128)(2,1)S(1)}, u32[]{:S(2)}, u32[]{:S(2)}) %collective-permute-start.3) | collective-permute-done | bytes 32800 | tf_op jit(solution)/shard_map/ppermute | solution.py:381
  103.8 4.0 %all-to-all-done.1.returned = f32[128,2,128]{2,1,0:T(2,128)S(1)} async-done(((f32[128,2,128]{2,1,0:T(2,128)}), f32[128,2,128]{2,1,0:T(2,128)S(1)}, u32[]{:S(2)}, u32[]{:S(2)}) %all-to-all-start.1) | async-done | bytes 131104 | tf_op jit(solution)/shard_map/all_to_all | solution.py:380
  107.8 0.0 copy-start.3
  107.8 0.9 copy-done.3
  108.7 0.0 copy-start.4
  108.7 0.8 copy-done.4
  109.6 1.4 %finish.1 = (bf16[64,64,128]{2,1,0:T(8,128)(2,1)}, f32[64,2,128]{2,1,0:T(2,128)}) custom-call(s32[64]{0:T(128)S(1)} %copy-done.5, f32[128,2,128]{2,1,0:T(2,128)S(1)} %all-to-all-done.1.returned, f32[64,2,128]{2,1,0:T(2,128)S(1)} %copy-done.4, f32[4,64,128]{2,1,0:T(8,128)S(1)} %copy-done.3, ...), custom_call_target="tpu_custom_call", output_to_operand_aliasing={{0}: (6, {})} | custom-call | tf_op jit(solution)/shard_map/finish/pallas_call | solution.py:341
Async XLA Ops:
  4.4 75.9 %copy-start = (bf16[4,128,128]{2,1,0:T(8,128)(2,1)S(1)}, bf16[4,128,128]{2,1,0:T(8,128)(2,1)}, u32[]{:S(2)}) copy-start(bf16[4,128,128]{2,1,0:T(8,128)(2,1)} %blend.1) | copy-start | bytes 393220
  4.4 75.9 %copy-start.1 = (bf16[4,128,128]{2,1,0:T(8,128)(2,1)S(1)}, bf16[4,128,128]{2,1,0:T(8,128)(2,1)}, u32[]{:S(2)}) copy-start(bf16[4,128,128]{2,1,0:T(8,128)(2,1)} %east.1) | copy-start | bytes 393220
  4.4 75.9 %copy-start.2 = (bf16[4,128,128]{2,1,0:T(8,128)(2,1)S(1)}, bf16[4,128,128]{2,1,0:T(8,128)(2,1)}, u32[]{:S(2)}) copy-start(bf16[4,128,128]{2,1,0:T(8,128)(2,1)} %north.1) | copy-start | bytes 393220
  4.4 75.9 %copy-start.5 = (s32[64]{0:T(128)S(1)}, s32[64]{0:T(128)}, u32[]{:S(2)}) copy-start(s32[64]{0:T(128)} %get-tuple-element.12.places) | copy-start | bytes 772
  4.4 75.9 %all-to-all-start = ((bf16[32,272,128]{2,1,0:T(8,128)(2,1)}), bf16[32,272,128]{2,1,0:T(8,128)(2,1)S(1)}, u32[]{:S(2)}, u32[]{:S(2)}) async-start(bf16[32,272,128]{2,1,0:T(8,128)(2,1)} %get-tuple-element.13), calls=%async_computation | async-start | bytes 4456448 | tf_op jit(solution)/shard_map/all_to_all | solution.py:374
  20.4 54.5 %collective-permute-start = (bf16[2,64,128]{2,1,0:T(8,128)(2,1)S(1)}, bf16[2,64,128]{2,1,0:T(8,128)(2,1)S(1)}, u32[]{:S(2)}, u32[]{:S(2)}) collective-permute-start(bf16[2,64,128]{2,1,0:T(8,128)(2,1)S(1)} %get-tuple-element.23), channel_id=1, source_target_pairs={{0,1},{1,2},{2,3},{3,4},{4,5},{5,6},{6,7},{7,8},{8,9},{9,10},{10,1... | collective-permute-start | bytes 98312 | tf_op jit(solution)/shard_map/ppermute | solution.py:375
  23.7 51.2 %collective-permute-start.1 = (bf16[2,64,128]{2,1,0:T(8,128)(2,1)S(1)}, bf16[2,64,128]{2,1,0:T(8,128)(2,1)S(1)}, u32[]{:S(2)}, u32[]{:S(2)}) collective-permute-start(bf16[2,64,128]{2,1,0:T(8,128)(2,1)S(1)} %get-tuple-element.22), channel_id=1, source_target_pairs={{1,0},{2,1},{3,2},{4,3},{5,4},{6,5},{7,6},{8,7},{9,8},{10,9},{11,1... | collective-permute-start | bytes 98312 | tf_op jit(solution)/shard_map/ppermute | solution.py:376
  74.9 5.4 %copy-start.6 = (bf16[2,64,128]{2,1,0:T(8,128)(2,1)}, bf16[2,64,128]{2,1,0:T(8,128)(2,1)S(1)}, u32[]{:S(2)}) copy-start(bf16[2,64,128]{2,1,0:T(8,128)(2,1)S(1)} %collective-permute-done.before) | copy-start | bytes 98308
  74.9 5.4 %copy-start.7 = (bf16[2,64,128]{2,1,0:T(8,128)(2,1)}, bf16[2,64,128]{2,1,0:T(8,128)(2,1)S(1)}, u32[]{:S(2)}) copy-start(bf16[2,64,128]{2,1,0:T(8,128)(2,1)S(1)} %collective-permute-done.1.after) | copy-start | bytes 98308
  87.6 20.2 %all-to-all-start.1 = ((f32[128,2,128]{2,1,0:T(2,128)}), f32[128,2,128]{2,1,0:T(2,128)S(1)}, u32[]{:S(2)}, u32[]{:S(2)}) async-start(f32[128,2,128]{2,1,0:T(2,128)} %get-tuple-element.14), calls=%async_computation.1 | async-start | bytes 262144 | tf_op jit(solution)/shard_map/all_to_all | solution.py:380
  94.0 8.3 %collective-permute-start.2 = (bf16[2,64,128]{2,1,0:T(8,128)(2,1)}, bf16[2,64,128]{2,1,0:T(8,128)(2,1)S(1)}, u32[]{:S(2)}, u32[]{:S(2)}) collective-permute-start(bf16[2,64,128]{2,1,0:T(8,128)(2,1)} %get-tuple-element.17), channel_id=1, source_target_pairs={{0,1},{1,2},{2,3},{3,4},{4,5},{5,6},{6,7},{7,8},{8,9},{9,10},{10,1... | collective-permute-start | bytes 98312 | tf_op jit(solution)/shard_map/ppermute | solution.py:382
  96.3 7.5 %collective-permute-start.3 = (bf16[2,64,128]{2,1,0:T(8,128)(2,1)}, bf16[2,64,128]{2,1,0:T(8,128)(2,1)S(1)}, u32[]{:S(2)}, u32[]{:S(2)}) collective-permute-start(bf16[2,64,128]{2,1,0:T(8,128)(2,1)} %get-tuple-element.18), channel_id=1, source_target_pairs={{1,0},{2,1},{3,2},{4,3},{5,4},{6,5},{7,6},{8,7},{9,8},{10,9},{11,1... | collective-permute-start | bytes 98312 | tf_op jit(solution)/shard_map/ppermute | solution.py:381
  107.8 0.9 copy-start.3
  108.7 0.8 copy-start.4

commit v3 on v2

--- a/solution.py
+++ b/solution.py
@@ -25,18 +25,31 @@
     return pltpu.with_memory_space_constraint(array, pltpu.VMEM)
 
 
-def pack_kernel(owner, step, column, kind, adjoint, send, places, codes, counts, tiles, meta, load_sem, sem, meta_sem):
+def pack_kernel(
+    owner_all, step_all, column_all, kind_all, adjoint, send, places,
+    owner, step, column, kind, codes, counts, tiles, meta, load_sem, sem, meta_sem,
+):
     tile_cols, tile_rows = owner.shape
     tiles_here, levels, _ = adjoint.shape
     lon_count = counts.shape[0]
     me = lax.axis_index("lon")
-    load = pltpu.make_async_copy(adjoint, tiles, load_sem)
+    asks = [
+        pltpu.make_async_copy(whole, here, load_sem.at[n])
+        for n, (whole, here) in enumerate(
+            ((owner_all, owner), (step_all, step), (column_all, column), (kind_all, kind))
+        )
+    ]
+    for ask in asks:
+        ask.start()
+    load = pltpu.make_async_copy(adjoint, tiles, load_sem.at[len(asks)])
     load.start()
 
     for d in range(lon_count):
         counts[d] = 0
         for r in range(CAP):
             codes[d * CAP + r] = 0
+    for ask in asks:
+        ask.wait()
 
     def place_rows(n, sent):
         for u in range(4):
@@ -77,7 +90,7 @@
             line = jnp.zeros((META, 128), jnp.int32)
             for r in range(CAP):
                 code = codes[d * CAP + r]
-                line = jnp.where(lane == r, jnp.where(code > EXACT, EXACT - code, code), line)
+                line = jnp.where(lane == me * CAP + r, jnp.where(code > EXACT, EXACT - code, code), line)
             meta[d] = line.astype(jnp.float32).astype(jnp.bfloat16)
         return carry
 
@@ -103,38 +116,56 @@
             pltpu.HBM((lon_count, CAP * levels + META, width), jnp.bfloat16),
             jax.ShapeDtypeStruct((tiles_here,), jnp.int32),
         ),
-        in_specs=[smem, smem, smem, smem, hbm],
+        in_specs=[hbm] * 5,
         out_specs=(hbm, smem),
         scratch_shapes=[
+            pltpu.SMEM(owner.shape, jnp.int32),
+            pltpu.SMEM(owner.shape, jnp.int32),
+            pltpu.SMEM(owner.shape, jnp.int32),
+            pltpu.SMEM(owner.shape, jnp.int32),
             pltpu.SMEM((lon_count * CAP,), jnp.int32),
             pltpu.SMEM((lon_count,), jnp.int32),
             pltpu.VMEM((tiles_here, levels, width), jnp.bfloat16),
             pltpu.VMEM((lon_count, META, width), jnp.bfloat16),
-            pltpu.SemaphoreType.DMA,
+            pltpu.SemaphoreType.DMA((5,)),
             pltpu.SemaphoreType.DMA,
             pltpu.SemaphoreType.DMA,
         ],
         compiler_params=pltpu.CompilerParams(vmem_limit_bytes=60 * 1024 * 1024),
         name="pack",
-    )(owner, step, column, kind, in_hbm(adjoint))
+    )(in_hbm(owner), in_hbm(step), in_hbm(column), in_hbm(kind), in_hbm(adjoint))
 
 
 def adjoint_kernel(
     places, received, adjoint, old, before, after, blend, east, north,
     result, edge_own, cross_before, cross_after, sensed_remote, sensed_home,
-    tiles, sources, sums, remote, home, rounded, edges, back, slopes, listed, codes, work, counts,
-    sem, code_sem, out_sem,
+    tiles, sources, sums, remote, home, rounded, edges, back, slopes, listed, codes, work, stay, counts, sem, code_sem, out_sem,
 ):
     lon_count = received.shape[0]
     tiles_here, levels, width = adjoint.shape
     slot_count = lon_count * CAP
     tile_cols = before.shape[0]
     block_count = tiles_here + 2 * tile_cols
-    room = work.shape[0] // (2 * KINDS)
+    room = slot_count + UNROLL
     me = lax.axis_index("lon")
 
-    line = received[:, CAP * levels : CAP * levels + META, :].astype(jnp.float32)[:, 0, :].astype(jnp.int32)
-    listed[...] = jnp.where(line < 0, EXACT - line, line)
+    line = received[:, CAP * levels : CAP * levels + META, :].astype(jnp.float32)[:, :8, :]
+    code = jnp.sum(line, axis=0).astype(jnp.int32)
+    code = jnp.where(code < 0, EXACT - code, code)
+    row = lax.broadcasted_iota(jnp.int32, (8, width), 0)
+    lane = lax.broadcasted_iota(jnp.int32, (8, width), 1)
+    source_device = lane // CAP
+    chosen = (code > 0) & (source_device != me) & (((code - 1) & (KINDS - 1)) == row)
+    member = chosen.astype(jnp.float32)
+    earlier = lax.broadcasted_iota(jnp.int32, (width, width), 0) < lax.broadcasted_iota(jnp.int32, (width, width), 1)
+    before_it = jnp.dot(
+        member.astype(jnp.bfloat16), earlier.astype(jnp.bfloat16), preferred_element_type=jnp.float32
+    ).astype(jnp.int32)
+    put_at = jnp.sum(jnp.where(chosen, row * room + before_it + 1, 0), axis=0, keepdims=True)
+    put_at = jnp.where(put_at > 0, put_at - 1, KINDS * room)
+    total = jnp.sum(member, axis=1, keepdims=True).astype(jnp.int32)
+    listed[0:8, :] = jnp.where(row == 0, put_at, jnp.where(row == 1, lane * CODES + code - 1, 0))
+    listed[8:16, :] = jnp.broadcast_to(total, (8, width))
     code_copy = pltpu.make_async_copy(listed, codes, code_sem)
     code_copy.start()
     loads = [
@@ -156,39 +187,29 @@
 
     lax.fori_loop(0, block_count + 1, clear, 0, unroll=3)
 
-    for k in range(2 * KINDS):
+    for k in range(KINDS):
         counts[k] = 0
-
-    def enlist(where, entry, code, valid):
-        row = where * KINDS + (code & (KINDS - 1))
-        n = counts[row]
-        work[row * room + n] = entry * CODES + code
-        counts[row] = n + valid.astype(jnp.int32)
 
     def enlist_home(n, carry):
         for u in range(8):
             place = places[n * 8 + u]
-            enlist(1, n * 8 + u, -place - 1, place < 0)
+            code = -place - 1
+            kind = code & (KINDS - 1)
+            count = counts[kind]
+            stay[kind * room + count] = (n * 8 + u) * CODES + code
+            counts[kind] = count + (place < 0).astype(jnp.int32)
         return carry
 
     lax.fori_loop(0, tiles_here // 8, enlist_home, 0)
     code_copy.wait()
-
-    def enlist_remote(n, carry):
-        for u in range(2):
-            s = n * 2 + u
-            for r in range(CAP):
-                code = codes[s, r]
-                enlist(0, s * CAP + r, code - 1, (code > 0) & (s != me))
-        return carry
-
-    lax.fori_loop(0, lon_count // 2, enlist_remote, 0)
+    for slot in range(slot_count):
+        work[codes[0, slot]] = codes[1, slot]
+    arrived_count = [codes[8 + k, 0] for k in range(KINDS)]
+    stay_count = [counts[k] for k in range(KINDS)]
     for k in range(KINDS):
-        for where, spare in ((0, slot_count), (1, tiles_here)):
-            row = where * KINDS + k
-            n = counts[row]
-            for u in range(UNROLL):
-                work[row * room + n + u] = spare * CODES + block_count * KINDS + k
+        for u in range(UNROLL):
+            work[k * room + arrived_count[k] + u] = slot_count * CODES + block_count * KINDS + k
+            stay[k * room + stay_count[k] + u] = tiles_here * CODES + block_count * KINDS + k
     for copy in loads:
         copy.wait()
 
@@ -200,8 +221,7 @@
     def home_tile(p):
         return tiles[jnp.minimum(p, tiles_here - 1)]
 
-    def some_tiles(row, kind, tile_at, sensed, n):
-        entries = [work[row * room + n * UNROLL + u] for u in range(UNROLL)]
+    def some_tiles(kind, entries, tile_at, sensed):
         place = [e // CODES for e in entries]
         block = [(e & (CODES - 1)) // KINDS for e in entries]
         arrived = [tile_at(p) for p in place]
@@ -211,21 +231,24 @@
         for u in range(UNROLL):
             full = arrived[u].astype(jnp.float32)
             s = slope[u * levels : (u + 1) * levels]
-            sensed[place[u], 0:1] = jnp.sum(full * s[:, :width], axis=0, keepdims=True)
-            sensed[place[u], 1:2] = jnp.sum(full * s[:, width:], axis=0, keepdims=True)
+            both = [jnp.sum(full * part, axis=0, keepdims=True) for part in (s[:, :width], s[:, width:])]
+            sensed[place[u]] = jnp.concatenate(both, axis=0).astype(sensed.dtype)
         for u in range(UNROLL):
             s = spread[u * levels : (u + 1) * levels]
             sums[block[u]] += s.astype(jnp.bfloat16).astype(jnp.float32)
 
-    for where, tile_at, sensed in ((0, arrived_tile, remote), (1, home_tile, home)):
+    for listing, many, tile_at, sensed in (
+        (work, arrived_count, arrived_tile, remote),
+        (stay, stay_count, home_tile, home),
+    ):
         for kind in range(KINDS):
-            row = where * KINDS + kind
-
-            def step(n, carry, row=row, kind=kind, tile_at=tile_at, sensed=sensed):
-                some_tiles(row, kind, tile_at, sensed, n)
+
+            def step(n, carry, kind=kind, listing=listing, tile_at=tile_at, sensed=sensed):
+                entries = [listing[kind * room + n * UNROLL + u] for u in range(UNROLL)]
+                some_tiles(kind, entries, tile_at, sensed)
                 return carry
 
-            lax.fori_loop(0, (counts[row] + UNROLL - 1) // UNROLL, step, 0)
+            lax.fori_loop(0, (many[kind] + UNROLL - 1) // UNROLL, step, 0)
 
     copies = []
 
@@ -236,22 +259,23 @@
 
     put(remote.at[pl.ds(0, slot_count)], sensed_remote)
     put(home.at[pl.ds(0, tiles_here)], sensed_home)
+    put(sums.at[pl.ds(tile_cols, tile_cols)], edge_own.at[pl.ds(0, tile_cols)])
+    put(sums.at[pl.ds(tiles_here, tile_cols)], edge_own.at[pl.ds(tile_cols, tile_cols)])
+
+    def finish(b, carry):
+        rounded[b] = sums[tile_cols + b].astype(jnp.bfloat16)
+        return carry
+
+    part = (tiles_here - 2 * tile_cols) // PARTS
+    for p in range(PARTS):
+        first = tile_cols + p * part
+        lax.fori_loop(first, first + part, finish, 0, unroll=3)
+        put(rounded.at[pl.ds(first, part)], result.at[pl.ds(first, part)])
     for c in range(tile_cols):
         edges[c] = sums[c].astype(jnp.bfloat16)
         edges[tile_cols + c] = sums[tile_cols + tiles_here + c].astype(jnp.bfloat16)
     put(edges.at[pl.ds(0, tile_cols)], cross_before)
     put(edges.at[pl.ds(tile_cols, tile_cols)], cross_after)
-    put(sums.at[pl.ds(tile_cols, tile_cols)], edge_own.at[pl.ds(0, tile_cols)])
-    put(sums.at[pl.ds(tiles_here, tile_cols)], edge_own.at[pl.ds(tile_cols, tile_cols)])
-
-    def finish(b, carry):
-        rounded[b] = sums[tile_cols + b].astype(jnp.bfloat16)
-        return carry
-
-    part = tiles_here // PARTS
-    for p in range(PARTS):
-        lax.fori_loop(p * part, (p + 1) * part, finish, 0, unroll=4)
-        put(rounded.at[pl.ds(p * part, part)], result.at[pl.ds(p * part, part)])
     for copy in copies:
         copy.wait()
 
@@ -263,6 +287,7 @@
     tile_cols = before.shape[0]
     block_count = tiles_here + 2 * tile_cols
     assert (block_count + 1) * KINDS <= CODES and block_count * KINDS <= EXACT + 256
+    assert slot_count == width and KINDS <= 8 and tiles_here <= slot_count
     smem = pl.BlockSpec(memory_space=pltpu.SMEM)
     vmem = pl.BlockSpec(memory_space=pltpu.VMEM)
     hbm = pl.BlockSpec(memory_space=pltpu.HBM)
@@ -274,7 +299,7 @@
             pltpu.HBM((2 * tile_cols, levels, width), jnp.float32),
             edge,
             edge,
-            pltpu.HBM((slot_count, 2, width), jnp.float32),
+            pltpu.HBM((slot_count, 2, width), jnp.bfloat16),
             pltpu.HBM((tiles_here, 2, width), jnp.float32),
         ),
         in_specs=[smem, vmem, hbm, hbm, hbm, hbm, vmem, vmem, vmem],
@@ -283,31 +308,60 @@
             pltpu.VMEM((tiles_here, levels, width), jnp.bfloat16),
             pltpu.VMEM((block_count, levels, width), jnp.bfloat16),
             pltpu.VMEM((block_count + 1, levels, width), jnp.float32),
-            pltpu.VMEM((slot_count + 1, 2, width), jnp.float32),
+            pltpu.VMEM((slot_count + 1, 2, width), jnp.bfloat16),
             pltpu.VMEM((tiles_here + 1, 2, width), jnp.float32),
             pltpu.VMEM((tiles_here, levels, width), jnp.bfloat16),
             pltpu.VMEM((2 * tile_cols, levels, width), jnp.bfloat16),
             pltpu.VMEM((KINDS, width, width), jnp.bfloat16),
             pltpu.VMEM((KINDS, width, 2 * width), jnp.bfloat16),
-            pltpu.VMEM((lon_count, width), jnp.int32),
-            pltpu.SMEM((lon_count, width), jnp.int32),
-            pltpu.SMEM((2 * KINDS * (slot_count + UNROLL),), jnp.int32),
-            pltpu.SMEM((2 * KINDS,), jnp.int32),
+            pltpu.VMEM((16, width), jnp.int32),
+            pltpu.SMEM((16, width), jnp.int32),
+            pltpu.SMEM((KINDS * (slot_count + UNROLL) + 1,), jnp.int32),
+            pltpu.SMEM((KINDS * (slot_count + UNROLL),), jnp.int32),
+            pltpu.SMEM((KINDS,), jnp.int32),
             pltpu.SemaphoreType.DMA((4,)),
             pltpu.SemaphoreType.DMA,
             pltpu.SemaphoreType.DMA((6 + PARTS,)),
         ],
         compiler_params=pltpu.CompilerParams(vmem_limit_bytes=VMEM_LIMIT),
         name="adjoint",
-    )(places, in_vmem(received), in_hbm(adjoint), in_hbm(old), in_hbm(before), in_hbm(after), blend, east, north)
-
-
-def finish_kernel(places, returned, sensed_home, edge_own, from_before, from_after, _, result, sensed, edges, out, sem):
+    )(places, received, in_hbm(adjoint), in_hbm(old), in_hbm(before), in_hbm(after), blend, east, north)
+
+
+def hold_kernel(edge_own, sensed_home, own, home, sem):
+    copies = [
+        pltpu.make_async_copy(edge_own, own, sem.at[0]),
+        pltpu.make_async_copy(sensed_home, home, sem.at[1]),
+    ]
+    for copy in copies:
+        copy.start()
+    for copy in copies:
+        copy.wait()
+
+
+def hold(edge_own, sensed_home):
+    vmem = pl.BlockSpec(memory_space=pltpu.VMEM)
+    hbm = pl.BlockSpec(memory_space=pltpu.HBM)
+    return pl.pallas_call(
+        hold_kernel,
+        out_shape=(
+            pltpu.VMEM(edge_own.shape, edge_own.dtype),
+            pltpu.VMEM(sensed_home.shape, sensed_home.dtype),
+        ),
+        in_specs=[hbm, hbm],
+        out_specs=(vmem, vmem),
+        scratch_shapes=[pltpu.SemaphoreType.DMA((2,))],
+        compiler_params=pltpu.CompilerParams(vmem_limit_bytes=8 * 1024 * 1024),
+        name="hold",
+    )(in_hbm(edge_own), in_hbm(sensed_home))
+
+
+def finish_kernel(places, returned, sensed_home, own, from_before, from_after, _, result, sensed, edges, out, sem):
     tiles_here = sensed.shape[0]
     tile_cols = from_before.shape[0]
     for c in range(tile_cols):
-        edges[c] = (edge_own[c] + from_before[c].astype(jnp.float32)).astype(jnp.bfloat16)
-        edges[tile_cols + c] = (edge_own[tile_cols + c] + from_after[c].astype(jnp.float32)).astype(jnp.bfloat16)
+        edges[c] = (own[c] + from_before[c].astype(jnp.float32)).astype(jnp.bfloat16)
+        edges[tile_cols + c] = (own[tile_cols + c] + from_after[c].astype(jnp.float32)).astype(jnp.bfloat16)
     copies = [
         pltpu.make_async_copy(edges.at[pl.ds(0, tile_cols)], result.at[pl.ds(0, tile_cols)], sem.at[0]),
         pltpu.make_async_copy(
@@ -324,7 +378,7 @@
         for u in range(8):
             t = n * 8 + u
             place = places[t]
-            out[t] = jnp.where(place < 0, sensed_home[t], returned[jnp.maximum(place, 0)])
+            out[t] = jnp.where(place < 0, sensed_home[t], returned[jnp.maximum(place, 0)].astype(jnp.float32))
         return carry
 
     lax.fori_loop(0, tiles_here // 8, place_some, 0)
@@ -333,28 +387,29 @@
         copy.wait()
 
 
-def finish(places, returned, sensed_home, edge_own, from_before, from_after, partial):
-    tiles_here, _, width = sensed_home.shape
+def finish(places, returned, sensed_home, own, from_before, from_after, partial):
+    tiles_here, levels, width = partial.shape
+    tile_cols = from_before.shape[0]
     smem = pl.BlockSpec(memory_space=pltpu.SMEM)
     vmem = pl.BlockSpec(memory_space=pltpu.VMEM)
     hbm = pl.BlockSpec(memory_space=pltpu.HBM)
     return pl.pallas_call(
         finish_kernel,
         out_shape=(
-            jax.ShapeDtypeStruct(partial.shape, partial.dtype),
-            jax.ShapeDtypeStruct((tiles_here, 2, width), jnp.float32),
+            pltpu.HBM(partial.shape, partial.dtype),
+            pltpu.HBM((tiles_here, 2, width), jnp.float32),
         ),
         in_specs=[smem] + [vmem] * 5 + [hbm],
         out_specs=(hbm, hbm),
         scratch_shapes=[
-            pltpu.VMEM(edge_own.shape, jnp.bfloat16),
+            pltpu.VMEM((2 * tile_cols, levels, width), jnp.bfloat16),
             pltpu.VMEM((tiles_here, 2, width), jnp.float32),
             pltpu.SemaphoreType.DMA((3,)),
         ],
         input_output_aliases={6: 0},
         compiler_params=pltpu.CompilerParams(vmem_limit_bytes=8 * 1024 * 1024),
         name="finish",
-    )(places, returned, sensed_home, edge_own, from_before, from_after, partial)
+    )(places, in_vmem(returned), in_vmem(sensed_home), in_vmem(own), from_before, from_after, partial)
 
 
 def on_device(
@@ -380,7 +435,8 @@
     returned = lax.all_to_all(sensed_remote, "lon", split_axis=0, concat_axis=0, tiled=True)
     from_after = lax.ppermute(cross_before, "lat", south_to_north)
     from_before = lax.ppermute(cross_after, "lat", north_to_south)
-    result, sensed = finish(places, returned, sensed_home, edge_own, from_before, from_after, partial)
+    own, home = hold(edge_own, sensed_home)
+    result, sensed = finish(places, returned, home, own, from_before, from_after, partial)
     return (
         result.reshape(tracer_old.shape),
         sensed.reshape(tile_rows, tile_cols, 2, width),

time: 112 us -> 108 us (0.964)
  waiting for transfers between devices: 57.8 us -> 55.6 us
  local copies, waits for them, and re-layouts: 2.56 us -> 0.82 us
    ppermute x1, waiting for transfers between devices: 46.5 us -> 37.2 us  [on_device(): before = lax.ppermute(old[-tile_cols:], 'lat', north_to_south)]
    ppermute x1, waiting for transfers between devices: 0.01 us -> 6.21 us  [on_device(): after = lax.ppermute(old[:tile_cols], 'lat', south_to_north)]
    all_to_all x1, waiting for transfers between devices: 5.36 us -> 8.49 us  [on_device(): lax.all_to_all(send, 'lon', split_axis=0, concat_axis=0, tiled=True)]
    unnamed x16 -> x12, local copies, waits for them, and re-layouts: 1.78 us -> 0.03 us
    all_to_all x1, waiting for transfers between devices: 4.01 us -> 2.65 us  [on_device(): lax.all_to_all(sensed_remote, 'lon', split_axis=0, concat_axis=0, tiled=T...]
    pallas_call x1 -> x2, Pallas kernels: 1.41 us -> 2.32 us  [the longest x1 1.4 us: finish(): pl.pallas_call(finish_kernel, out_shape=(pltpu.HBM(partial.shape, partial...]
  transfers between devices with their start and end apart: 6 -> 6, of which waited for: 5 -> 5; matrix products, arithmetic and copies ran while one was open for 1% -> 1% of each run, Pallas kernels for 0% -> 1%
where the time goes in v3:
time: 108 us
  waiting for transfers between devices  55.6 us (51%)
  starting transfers between devices  37.9 us (35%)
  Pallas kernels  12.6 us (12%)
    ppermute x1, waiting for transfers between devices, on_device(): before = lax.ppermute(old[-tile_cols:], 'lat', north_to_south)  37.2 us
    all_to_all x1, starting transfers between devices, on_device(): lax.all_to_all(send, 'lon', split_axis=0, concat_axis=0, tiled=True)  15.2 us
    all_to_all x1, waiting for transfers between devices, on_device(): lax.all_to_all(send, 'lon', split_axis=0, concat_axis=0, tiled=True)  8.49 us
    pallas_call x1, Pallas kernels, adjoint_step(): pl.pallas_call(adjoint_kernel, out_shape=(pltpu.HBM((tiles_here, levels,...  6.98 us
    all_to_all x1, starting transfers between devices, on_device(): lax.all_to_all(sensed_remote, 'lon', split_axis=0, concat_axis=0, tiled=T...  6.81 us
    ppermute x1, waiting for transfers between devices, on_device(): after = lax.ppermute(old[:tile_cols], 'lat', south_to_north)  6.21 us
    ppermute x1, starting transfers between devices, on_device(): from_after = lax.ppermute(cross_before, 'lat', south_to_north)  5.34 us
    ppermute x1, starting transfers between devices, on_device(): after = lax.ppermute(old[:tile_cols], 'lat', south_to_north)  4.55 us
  transfers between devices with their start and end apart: 6, of which 5 were waited for; matrix products, arithmetic and copies ran while one was open for 1% of the time, Pallas kernels for 1%

profile of v3, /device:TPU:8, one launch (start us, length us, event | category | flops | bytes accessed | tf_op | source)
XLA Modules:
  0.0 107.7 jit_solution(465797455541811064)
XLA Ops:
  0.6 3.3 %pack.1 = (bf16[32,272,128]{2,1,0:T(8,128)(2,1)}, s32[64]{0:T(128)}) custom-call(s32[2,32]{1,0:T(2,128)} %bitcast.16, s32[2,32]{1,0:T(2,128)} %bitcast.17, s32[2,32]{1,0:T(2,128)} %bitcast.18, s32[2,32]{1,0:T(2,128)} %bitcast.19, bf16[64,64,128]{2,1,0:T(8,128)(2,1)} %bitcast.12), custom_call_target="tpu_custom_call" | custom-call | tf_op jit(solution)/shard_map/pack/pallas_call | solution.py:113
  3.9 0.0 copy-start
  4.0 0.0 copy-start.1
  4.0 0.0 copy-start.2
  4.0 0.0 copy-start.3
  4.0 15.2 %all-to-all-start = ((bf16[32,272,128]{2,1,0:T(8,128)(2,1)}), bf16[32,272,128]{2,1,0:T(8,128)(2,1)S(1)}, u32[]{:S(2)}, u32[]{:S(2)}) async-start(bf16[32,272,128]{2,1,0:T(8,128)(2,1)} %get-tuple-element.15), calls=%async_computation | async-start | bytes 4456448 | tf_op jit(solution)/shard_map/all_to_all | solution.py:429
  19.2 0.8 slice_bitcast_fusion
  20.0 3.4 %collective-permute-start = (bf16[2,64,128]{2,1,0:T(8,128)(2,1)S(1)}, bf16[2,64,128]{2,1,0:T(8,128)(2,1)S(1)}, u32[]{:S(2)}, u32[]{:S(2)}) collective-permute-start(bf16[2,64,128]{2,1,0:T(8,128)(2,1)S(1)} %get-tuple-element.27), channel_id=1, source_target_pairs={{0,1},{1,2},{2,3},{3,4},{4,5},{5,6},{6,7},{7,8},{8,9},{9,10},{10,1... | collective-permute-start | bytes 98312 | tf_op jit(solution)/shard_map/ppermute | solution.py:430
  23.4 4.6 %collective-permute-start.1 = (bf16[2,64,128]{2,1,0:T(8,128)(2,1)S(1)}, bf16[2,64,128]{2,1,0:T(8,128)(2,1)S(1)}, u32[]{:S(2)}, u32[]{:S(2)}) collective-permute-start(bf16[2,64,128]{2,1,0:T(8,128)(2,1)S(1)} %get-tuple-element.26), channel_id=1, source_target_pairs={{1,0},{2,1},{3,2},{4,3},{5,4},{6,5},{7,6},{8,7},{9,8},{10,9},{11,1... | collective-permute-start | bytes 98312 | tf_op jit(solution)/shard_map/ppermute | solution.py:431
  28.0 37.2 %collective-permute-done.before = bf16[2,64,128]{2,1,0:T(8,128)(2,1)S(1)} collective-permute-done((bf16[2,64,128]{2,1,0:T(8,128)(2,1)S(1)}, bf16[2,64,128]{2,1,0:T(8,128)(2,1)S(1)}, u32[]{:S(2)}, u32[]{:S(2)}) %collective-permute-start) | collective-permute-done | bytes 32800 | tf_op jit(solution)/shard_map/ppermute | solution.py:430
  65.2 0.0 copy-start.4
  65.2 6.2 %collective-permute-done.1.after = bf16[2,64,128]{2,1,0:T(8,128)(2,1)S(1)} collective-permute-done((bf16[2,64,128]{2,1,0:T(8,128)(2,1)S(1)}, bf16[2,64,128]{2,1,0:T(8,128)(2,1)S(1)}, u32[]{:S(2)}, u32[]{:S(2)}) %collective-permute-start.1) | collective-permute-done | bytes 32800 | tf_op jit(solution)/shard_map/ppermute | solution.py:431
  71.4 0.0 copy-start.5
  71.4 8.5 %all-to-all-done.received = bf16[32,272,128]{2,1,0:T(8,128)(2,1)S(1)} async-done(((bf16[32,272,128]{2,1,0:T(8,128)(2,1)}), bf16[32,272,128]{2,1,0:T(8,128)(2,1)S(1)}, u32[]{:S(2)}, u32[]{:S(2)}) %all-to-all-start) | async-done | bytes 2228256 | tf_op jit(solution)/shard_map/all_to_all | solution.py:429
  79.9 0.0 copy-done.4
  79.9 0.0 copy-done.5
  79.9 0.0 copy-done
  79.9 0.0 copy-done.1
  79.9 0.0 copy-done.2
  79.9 0.0 copy-done.3
  79.9 7.0 %adjoint.1 = (bf16[64,64,128]{2,1,0:T(8,128)(2,1)}, f32[4,64,128]{2,1,0:T(8,128)}, bf16[2,64,128]{2,1,0:T(8,128)(2,1)}, bf16[2,64,128]{2,1,0:T(8,128)(2,1)}, bf1...) custom-call(s32[64]{0:T(128)S(1)} %copy-done.3, bf16[32,272,128]{2,1,0:T(8,128)(2,1)S(1)} %all-to-all-done.received, ...), custom_call_target="tpu_custom_call" | custom-call | tf_op jit(solution)/shard_map/adjoint/pallas_call | solution.py:295
  86.9 6.8 %all-to-all-start.1 = ((bf16[128,2,128]{2,1,0:T(2,128)(2,1)}), bf16[128,2,128]{2,1,0:T(2,128)(2,1)S(1)}, u32[]{:S(2)}, u32[]{:S(2)}) async-start(bf16[128,2,128]{2,1,0:T(2,128)(2,1)} %get-tuple-element.16), calls=%async_computation.1 | async-start | bytes 131072 | tf_op jit(solution)/shard_map/all_to_all | solution.py:435
  93.8 2.6 %collective-permute-start.2 = (bf16[2,64,128]{2,1,0:T(8,128)(2,1)}, bf16[2,64,128]{2,1,0:T(8,128)(2,1)S(1)}, u32[]{:S(2)}, u32[]{:S(2)}) collective-permute-start(bf16[2,64,128]{2,1,0:T(8,128)(2,1)} %get-tuple-element.21), channel_id=1, source_target_pairs={{0,1},{1,2},{2,3},{3,4},{4,5},{5,6},{6,7},{7,8},{8,9},{9,10},{10,1... | collective-permute-start | bytes 98312 | tf_op jit(solution)/shard_map/ppermute | solution.py:437
  96.4 5.3 %collective-permute-start.3 = (bf16[2,64,128]{2,1,0:T(8,128)(2,1)}, bf16[2,64,128]{2,1,0:T(8,128)(2,1)S(1)}, u32[]{:S(2)}, u32[]{:S(2)}) collective-permute-start(bf16[2,64,128]{2,1,0:T(8,128)(2,1)} %get-tuple-element.22), channel_id=1, source_target_pairs={{1,0},{2,1},{3,2},{4,3},{5,4},{6,5},{7,6},{8,7},{9,8},{10,9},{11,1... | collective-permute-start | bytes 98312 | tf_op jit(solution)/shard_map/ppermute | solution.py:436
  101.7 0.9 hold.1
  102.7 0.0 collective-permute-done.2.from_before
  102.7 0.9 collective-permute-done.3.from_after
  103.6 2.7 %all-to-all-done.1.returned = bf16[128,2,128]{2,1,0:T(2,128)(2,1)S(1)} async-done(((bf16[128,2,128]{2,1,0:T(2,128)(2,1)}), bf16[128,2,128]{2,1,0:T(2,128)(2,1)S(1)}, u32[]{:S(2)}, u32[]{:S(2)}) %all-to-all-start.1) | async-done | bytes 65568 | tf_op jit(solution)/shard_map/all_to_all | solution.py:435
  106.3 1.4 %finish.1 = (bf16[64,64,128]{2,1,0:T(8,128)(2,1)}, f32[64,2,128]{2,1,0:T(2,128)}) custom-call(s32[64]{0:T(128)S(1)} %copy-done.3, bf16[128,2,128]{2,1,0:T(2,128)(2,1)S(1)} %all-to-all-done.1.returned, f32[64,2,128]{2,1,0:T(2,128)S(1)} %get-tuple-element.19.sensed_home, f32[4,64,128]{2,1,0:T(8,128)S(1)} %get-tuple-element.20.own, ...), custom_call_target="tpu_custom_call", output_to_operand_aliasing={{0}: (6, {})} | custom-call | tf_op jit(solution)/shard_map/finish/pallas_call | solution.py:396
Async XLA Ops:
  3.9 76.0 %copy-start = (bf16[4,128,128]{2,1,0:T(8,128)(2,1)S(1)}, bf16[4,128,128]{2,1,0:T(8,128)(2,1)}, u32[]{:S(2)}) copy-start(bf16[4,128,128]{2,1,0:T(8,128)(2,1)} %blend.1) | copy-start | bytes 393220
  4.0 76.0 %copy-start.1 = (bf16[4,128,128]{2,1,0:T(8,128)(2,1)S(1)}, bf16[4,128,128]{2,1,0:T(8,128)(2,1)}, u32[]{:S(2)}) copy-start(bf16[4,128,128]{2,1,0:T(8,128)(2,1)} %east.1) | copy-start | bytes 393220
  4.0 76.0 %copy-start.2 = (bf16[4,128,128]{2,1,0:T(8,128)(2,1)S(1)}, bf16[4,128,128]{2,1,0:T(8,128)(2,1)}, u32[]{:S(2)}) copy-start(bf16[4,128,128]{2,1,0:T(8,128)(2,1)} %north.1) | copy-start | bytes 393220
  4.0 76.0 %copy-start.3 = (s32[64]{0:T(128)S(1)}, s32[64]{0:T(128)}, u32[]{:S(2)}) copy-start(s32[64]{0:T(128)} %get-tuple-element.14.places) | copy-start | bytes 772
  4.0 75.9 %all-to-all-start = ((bf16[32,272,128]{2,1,0:T(8,128)(2,1)}), bf16[32,272,128]{2,1,0:T(8,128)(2,1)S(1)}, u32[]{:S(2)}, u32[]{:S(2)}) async-start(bf16[32,272,128]{2,1,0:T(8,128)(2,1)} %get-tuple-element.15), calls=%async_computation | async-start | bytes 4456448 | tf_op jit(solution)/shard_map/all_to_all | solution.py:429
  20.0 45.2 %collective-permute-start = (bf16[2,64,128]{2,1,0:T(8,128)(2,1)S(1)}, bf16[2,64,128]{2,1,0:T(8,128)(2,1)S(1)}, u32[]{:S(2)}, u32[]{:S(2)}) collective-permute-start(bf16[2,64,128]{2,1,0:T(8,128)(2,1)S(1)} %get-tuple-element.27), channel_id=1, source_target_pairs={{0,1},{1,2},{2,3},{3,4},{4,5},{5,6},{6,7},{7,8},{8,9},{9,10},{10,1... | collective-permute-start | bytes 98312 | tf_op jit(solution)/shard_map/ppermute | solution.py:430
  23.4 48.0 %collective-permute-start.1 = (bf16[2,64,128]{2,1,0:T(8,128)(2,1)S(1)}, bf16[2,64,128]{2,1,0:T(8,128)(2,1)S(1)}, u32[]{:S(2)}, u32[]{:S(2)}) collective-permute-start(bf16[2,64,128]{2,1,0:T(8,128)(2,1)S(1)} %get-tuple-element.26), channel_id=1, source_target_pairs={{1,0},{2,1},{3,2},{4,3},{5,4},{6,5},{7,6},{8,7},{9,8},{10,9},{11,1... | collective-permute-start | bytes 98312 | tf_op jit(solution)/shard_map/ppermute | solution.py:431
  65.2 14.7 %copy-start.4 = (bf16[2,64,128]{2,1,0:T(8,128)(2,1)}, bf16[2,64,128]{2,1,0:T(8,128)(2,1)S(1)}, u32[]{:S(2)}) copy-start(bf16[2,64,128]{2,1,0:T(8,128)(2,1)S(1)} %collective-permute-done.before) | copy-start | bytes 98308
  71.4 8.5 %copy-start.5 = (bf16[2,64,128]{2,1,0:T(8,128)(2,1)}, bf16[2,64,128]{2,1,0:T(8,128)(2,1)S(1)}, u32[]{:S(2)}) copy-start(bf16[2,64,128]{2,1,0:T(8,128)(2,1)S(1)} %collective-permute-done.1.after) | copy-start | bytes 98308
  86.9 19.3 %all-to-all-start.1 = ((bf16[128,2,128]{2,1,0:T(2,128)(2,1)}), bf16[128,2,128]{2,1,0:T(2,128)(2,1)S(1)}, u32[]{:S(2)}, u32[]{:S(2)}) async-start(bf16[128,2,128]{2,1,0:T(2,128)(2,1)} %get-tuple-element.16), calls=%async_computation.1 | async-start | bytes 131072 | tf_op jit(solution)/shard_map/all_to_all | solution.py:435
  93.8 8.9 %collective-permute-start.2 = (bf16[2,64,128]{2,1,0:T(8,128)(2,1)}, bf16[2,64,128]{2,1,0:T(8,128)(2,1)S(1)}, u32[]{:S(2)}, u32[]{:S(2)}) collective-permute-start(bf16[2,64,128]{2,1,0:T(8,128)(2,1)} %get-tuple-element.21), channel_id=1, source_target_pairs={{0,1},{1,2},{2,3},{3,4},{4,5},{5,6},{6,7},{7,8},{8,9},{9,10},{10,1... | collective-permute-start | bytes 98312 | tf_op jit(solution)/shard_map/ppermute | solution.py:437
  96.4 7.2 %collective-permute-start.3 = (bf16[2,64,128]{2,1,0:T(8,128)(2,1)}, bf16[2,64,128]{2,1,0:T(8,128)(2,1)S(1)}, u32[]{:S(2)}, u32[]{:S(2)}) collective-permute-start(bf16[2,64,128]{2,1,0:T(8,128)(2,1)} %get-tuple-element.22), channel_id=1, source_target_pairs={{1,0},{2,1},{3,2},{4,3},{5,4},{6,5},{7,6},{8,7},{9,8},{10,9},{11,1... | collective-permute-start | bytes 98312 | tf_op jit(solution)/shard_map/ppermute | solution.py:436

commit v4 on v3

--- a/solution.py
+++ b/solution.py
@@ -12,7 +12,7 @@
 KINDS = 4
 CODES = 512
 EXACT = 200
-UNROLL = 8
+UNROLL = 12
 PARTS = 4
 VMEM_LIMIT = 24 * 1024 * 1024
 
@@ -50,51 +50,41 @@
             codes[d * CAP + r] = 0
     for ask in asks:
         ask.wait()
-
-    def place_rows(n, sent):
+    load.wait()
+
+    def send_rows(n, sent):
         for u in range(4):
             i = n * 4 + u
             for j in range(tile_cols):
+                tile = i * tile_cols + j
                 to = owner[j, i]
                 rank = counts[to]
                 remote = to != me
                 counts[to] = rank + 1
-                block = (i + step[j, i]) * tile_cols + column[j, i]
-                code = block * KINDS + kind[j, i] + 1
-                places[i * tile_cols + j] = jnp.where(remote, to * CAP + rank, -code)
-                codes[jnp.where(remote, to * CAP + rank, me * CAP)] = jnp.where(remote, code, 0)
+                code = ((i + step[j, i]) * tile_cols + column[j, i]) * KINDS + kind[j, i] + 1
+                slot = to * CAP + rank
+                places[tile] = jnp.where(remote, slot, -code)
+                codes[jnp.where(remote, slot, me * CAP)] = jnp.where(remote, code, 0)
+
+                @pl.when(remote)
+                def _():
+                    rows = pl.ds(pl.multiple_of(rank * levels, levels), levels)
+                    pltpu.make_async_copy(tiles.at[tile], send.at[to, rows, :], sem).start()
+
                 sent = sent + remote.astype(jnp.int32)
         return sent
 
-    sent = lax.fori_loop(0, tile_rows // 4, place_rows, 0)
-    load.wait()
-
-    def send_rows(n, carry):
-        for u in range(8):
-            tile = n * 8 + u
-            slot = places[tile]
-
-            @pl.when(slot >= 0)
-            def _():
-                rows = pl.ds(pl.multiple_of((slot & (CAP - 1)) * levels, levels), levels)
-                pltpu.make_async_copy(tiles.at[tile], send.at[slot // CAP, rows, :], sem).start()
-
-        return carry
-
-    lax.fori_loop(0, tiles_here // 8, send_rows, 0)
-    lane = lax.broadcasted_iota(jnp.int32, (META, 128), 1)
-
-    def describe(n, carry):
-        for u in range(4):
-            d = n * 4 + u
-            line = jnp.zeros((META, 128), jnp.int32)
-            for r in range(CAP):
-                code = codes[d * CAP + r]
-                line = jnp.where(lane == me * CAP + r, jnp.where(code > EXACT, EXACT - code, code), line)
-            meta[d] = line.astype(jnp.float32).astype(jnp.bfloat16)
-        return carry
-
-    lax.fori_loop(0, lon_count // 4, describe, 0)
+    sent = lax.fori_loop(0, tile_rows // 4, send_rows, 0)
+    lane = lax.broadcasted_iota(jnp.int32, (8, meta.shape[2]), 1)
+    lines = [jnp.zeros(lane.shape, jnp.int32)] * CAP
+    for d in range(lon_count):
+        for r in range(CAP):
+            lines[r] = jnp.where(lane == d * CAP + r, codes[d * CAP + r], lines[r])
+    line = sum(lines[1:], lines[0])
+    line = jnp.where(line > EXACT, EXACT - line, line).astype(jnp.float32)
+    line = jnp.concatenate([line, line], axis=0).astype(jnp.bfloat16)
+    for d in range(lon_count):
+        meta[d] = line
     told = pltpu.make_async_copy(meta, send.at[:, pl.ds(CAP * levels, META), :], meta_sem)
     told.start()
 
@@ -137,9 +127,9 @@
 
 
 def adjoint_kernel(
-    places, received, adjoint, old, before, after, blend, east, north,
+    places_all, received, adjoint, old, before, after, blend_all, east_all, north_all,
     result, edge_own, cross_before, cross_after, sensed_remote, sensed_home,
-    tiles, sources, sums, remote, home, rounded, edges, back, slopes, listed, codes, work, stay, counts, sem, code_sem, out_sem,
+    tiles, sources, sums, remote, home, rounded, edges, blend, back, slopes, listed, places, codes, work, stay, counts, sem, code_sem, out_sem,
 ):
     lon_count = received.shape[0]
     tiles_here, levels, width = adjoint.shape
@@ -149,15 +139,22 @@
     room = slot_count + UNROLL
     me = lax.axis_index("lon")
 
-    line = received[:, CAP * levels : CAP * levels + META, :].astype(jnp.float32)[:, :8, :]
-    code = jnp.sum(line, axis=0).astype(jnp.int32)
+    told = received[:, CAP * levels : CAP * levels + META, :].astype(jnp.float32)[:, 0, :]
+    device = lax.broadcasted_iota(jnp.int32, (lon_count, width), 0)
+    spot = lax.broadcasted_iota(jnp.int32, (lon_count, width), 1)
+    told = jnp.where(spot // CAP == me, told, 0.0).astype(jnp.bfloat16)
+    first = lax.broadcasted_iota(jnp.int32, (width, width), 0)
+    second = lax.broadcasted_iota(jnp.int32, (width, width), 1)
+    again = ((first - second) % CAP == 0).astype(jnp.bfloat16)
+    asked = jnp.dot(told, again, preferred_element_type=jnp.float32)
+    code = jnp.sum(jnp.where(spot // CAP == device, asked, 0.0), axis=0, keepdims=True).astype(jnp.int32)
     code = jnp.where(code < 0, EXACT - code, code)
     row = lax.broadcasted_iota(jnp.int32, (8, width), 0)
     lane = lax.broadcasted_iota(jnp.int32, (8, width), 1)
     source_device = lane // CAP
     chosen = (code > 0) & (source_device != me) & (((code - 1) & (KINDS - 1)) == row)
     member = chosen.astype(jnp.float32)
-    earlier = lax.broadcasted_iota(jnp.int32, (width, width), 0) < lax.broadcasted_iota(jnp.int32, (width, width), 1)
+    earlier = first < second
     before_it = jnp.dot(
         member.astype(jnp.bfloat16), earlier.astype(jnp.bfloat16), preferred_element_type=jnp.float32
     ).astype(jnp.int32)
@@ -174,18 +171,26 @@
         pltpu.make_async_copy(after, sources.at[pl.ds(tile_cols + tiles_here, tile_cols)], sem.at[2]),
         pltpu.make_async_copy(adjoint, tiles, sem.at[3]),
     ]
+    weights = [
+        pltpu.make_async_copy(blend_all, blend, sem.at[4]),
+        pltpu.make_async_copy(east_all, slopes.at[:, :, pl.ds(0, width)], sem.at[5]),
+        pltpu.make_async_copy(north_all, slopes.at[:, :, pl.ds(width, width)], sem.at[6]),
+        pltpu.make_async_copy(places_all, places, sem.at[7]),
+    ]
+    for copy in weights:
+        copy.start()
     for copy in loads:
         copy.start()
-    for k in range(KINDS):
-        back[k] = blend[k].T
-        slopes[k, :, :width] = east[k]
-        slopes[k, :, width:] = north[k]
-
     def clear(b, carry):
         sums[b] = jnp.zeros((levels, width), jnp.float32)
         return carry
 
     lax.fori_loop(0, block_count + 1, clear, 0, unroll=3)
+
+    for copy in weights:
+        copy.wait()
+    for k in range(KINDS):
+        back[k] = blend[k].T
 
     for k in range(KINDS):
         counts[k] = 0
@@ -210,7 +215,7 @@
         for u in range(UNROLL):
             work[k * room + arrived_count[k] + u] = slot_count * CODES + block_count * KINDS + k
             stay[k * room + stay_count[k] + u] = tiles_here * CODES + block_count * KINDS + k
-    for copy in loads:
+    for copy in loads[:3]:
         copy.wait()
 
     def arrived_tile(p):
@@ -237,10 +242,12 @@
             s = spread[u * levels : (u + 1) * levels]
             sums[block[u]] += s.astype(jnp.bfloat16).astype(jnp.float32)
 
-    for listing, many, tile_at, sensed in (
+    for where, (listing, many, tile_at, sensed) in enumerate((
         (work, arrived_count, arrived_tile, remote),
         (stay, stay_count, home_tile, home),
-    ):
+    )):
+        if where == 1:
+            loads[3].wait()
         for kind in range(KINDS):
 
             def step(n, carry, kind=kind, listing=listing, tile_at=tile_at, sensed=sensed):
@@ -288,7 +295,6 @@
     block_count = tiles_here + 2 * tile_cols
     assert (block_count + 1) * KINDS <= CODES and block_count * KINDS <= EXACT + 256
     assert slot_count == width and KINDS <= 8 and tiles_here <= slot_count
-    smem = pl.BlockSpec(memory_space=pltpu.SMEM)
     vmem = pl.BlockSpec(memory_space=pltpu.VMEM)
     hbm = pl.BlockSpec(memory_space=pltpu.HBM)
     edge = pltpu.HBM((tile_cols, levels, width), jnp.bfloat16)
@@ -302,7 +308,7 @@
             pltpu.HBM((slot_count, 2, width), jnp.bfloat16),
             pltpu.HBM((tiles_here, 2, width), jnp.float32),
         ),
-        in_specs=[smem, vmem, hbm, hbm, hbm, hbm, vmem, vmem, vmem],
+        in_specs=[hbm, vmem] + [hbm] * 7,
         out_specs=(hbm,) * 6,
         scratch_shapes=[
             pltpu.VMEM((tiles_here, levels, width), jnp.bfloat16),
@@ -313,19 +319,24 @@
             pltpu.VMEM((tiles_here, levels, width), jnp.bfloat16),
             pltpu.VMEM((2 * tile_cols, levels, width), jnp.bfloat16),
             pltpu.VMEM((KINDS, width, width), jnp.bfloat16),
+            pltpu.VMEM((KINDS, width, width), jnp.bfloat16),
             pltpu.VMEM((KINDS, width, 2 * width), jnp.bfloat16),
             pltpu.VMEM((16, width), jnp.int32),
+            pltpu.SMEM((tiles_here,), jnp.int32),
             pltpu.SMEM((16, width), jnp.int32),
             pltpu.SMEM((KINDS * (slot_count + UNROLL) + 1,), jnp.int32),
             pltpu.SMEM((KINDS * (slot_count + UNROLL),), jnp.int32),
             pltpu.SMEM((KINDS,), jnp.int32),
-            pltpu.SemaphoreType.DMA((4,)),
+            pltpu.SemaphoreType.DMA((8,)),
             pltpu.SemaphoreType.DMA,
             pltpu.SemaphoreType.DMA((6 + PARTS,)),
         ],
         compiler_params=pltpu.CompilerParams(vmem_limit_bytes=VMEM_LIMIT),
         name="adjoint",
-    )(places, received, in_hbm(adjoint), in_hbm(old), in_hbm(before), in_hbm(after), blend, east, north)
+    )(
+        in_hbm(places), received, in_hbm(adjoint), in_hbm(old), in_hbm(before), in_hbm(after),
+        in_hbm(blend), in_hbm(east), in_hbm(north),
+    )
 
 
 def hold_kernel(edge_own, sensed_home, own, home, sem):
@@ -356,7 +367,11 @@
     )(in_hbm(edge_own), in_hbm(sensed_home))
 
 
-def finish_kernel(places, returned, sensed_home, own, from_before, from_after, _, result, sensed, edges, out, sem):
+def finish_kernel(
+    places_all, returned, sensed_home, own, from_before, from_after, _, result, sensed, edges, out, places, sem
+):
+    where = pltpu.make_async_copy(places_all, places, sem.at[3])
+    where.start()
     tiles_here = sensed.shape[0]
     tile_cols = from_before.shape[0]
     for c in range(tile_cols):
@@ -373,6 +388,7 @@
     ]
     copies[0].start()
     copies[1].start()
+    where.wait()
 
     def place_some(n, carry):
         for u in range(8):
@@ -390,7 +406,6 @@
 def finish(places, returned, sensed_home, own, from_before, from_after, partial):
     tiles_here, levels, width = partial.shape
     tile_cols = from_before.shape[0]
-    smem = pl.BlockSpec(memory_space=pltpu.SMEM)
     vmem = pl.BlockSpec(memory_space=pltpu.VMEM)
     hbm = pl.BlockSpec(memory_space=pltpu.HBM)
     return pl.pallas_call(
@@ -399,17 +414,18 @@
             pltpu.HBM(partial.shape, partial.dtype),
             pltpu.HBM((tiles_here, 2, width), jnp.float32),
         ),
-        in_specs=[smem] + [vmem] * 5 + [hbm],
+        in_specs=[hbm] + [vmem] * 5 + [hbm],
         out_specs=(hbm, hbm),
         scratch_shapes=[
             pltpu.VMEM((2 * tile_cols, levels, width), jnp.bfloat16),
             pltpu.VMEM((tiles_here, 2, width), jnp.float32),
-            pltpu.SemaphoreType.DMA((3,)),
+            pltpu.SMEM((tiles_here,), jnp.int32),
+            pltpu.SemaphoreType.DMA((4,)),
         ],
         input_output_aliases={6: 0},
         compiler_params=pltpu.CompilerParams(vmem_limit_bytes=8 * 1024 * 1024),
         name="finish",
-    )(places, in_vmem(returned), in_vmem(sensed_home), in_vmem(own), from_before, from_after, partial)
+    )(in_hbm(places), in_vmem(returned), in_vmem(sensed_home), in_vmem(own), from_before, from_after, partial)
 
 
 def on_device(

time: 108 us -> 107 us (level)
    ppermute x1, waiting for transfers between devices: 37.2 us -> 47.5 us  [on_device(): before = lax.ppermute(old[-tile_cols:], 'lat', north_to_south)]
    ppermute x1, waiting for transfers between devices: 6.21 us -> 0.01 us  [on_device(): after = lax.ppermute(old[:tile_cols], 'lat', south_to_north)]
    all_to_all x1, waiting for transfers between devices: 8.49 us -> 4.41 us  [on_device(): lax.all_to_all(send, 'lon', split_axis=0, concat_axis=0, tiled=True)]
  transfers between devices with their start and end apart: 6 -> 6, of which waited for: 5 -> 4; matrix products, arithmetic and copies ran while one was open for 1% -> 1% of each run, Pallas kernels for 1% -> 1%
where the time goes in v4:
time: 107 us; the launch traced here: 106 us
  waiting for transfers between devices  55.7 us (52%)
  starting transfers between devices  37.6 us (35%)
  Pallas kernels  11.6 us (11%)
    ppermute x1, waiting for transfers between devices, on_device(): before = lax.ppermute(old[-tile_cols:], 'lat', north_to_south)  47.5 us
    all_to_all x1, starting transfers between devices, on_device(): lax.all_to_all(send, 'lon', split_axis=0, concat_axis=0, tiled=True)  15.1 us
    all_to_all x1, starting transfers between devices, on_device(): lax.all_to_all(sensed_remote, 'lon', split_axis=0, concat_axis=0, tiled=T...  6.67 us
    pallas_call x1, Pallas kernels, adjoint_step(): pl.pallas_call(adjoint_kernel, out_shape=(pltpu.HBM((tiles_here, levels,...  6.05 us
    ppermute x1, starting transfers between devices, on_device(): from_after = lax.ppermute(cross_before, 'lat', south_to_north)  5.43 us
    ppermute x1, starting transfers between devices, on_device(): after = lax.ppermute(old[:tile_cols], 'lat', south_to_north)  4.64 us
    all_to_all x1, waiting for transfers between devices, on_device(): lax.all_to_all(send, 'lon', split_axis=0, concat_axis=0, tiled=True)  4.41 us
    ppermute x1, starting transfers between devices, on_device(): before = lax.ppermute(old[-tile_cols:], 'lat', north_to_south)  3.3 us
  transfers between devices with their start and end apart: 6, of which 4 were waited for; matrix products, arithmetic and copies ran while one was open for 1% of the time, Pallas kernels for 1%

profile of v4, /device:TPU:8, one launch (start us, length us, event | category | flops | bytes accessed | tf_op | source)
XLA Modules:
  0.0 106.4 jit_solution(10122407595243437351)
XLA Ops:
  0.6 3.1 %pack.1 = (bf16[32,272,128]{2,1,0:T(8,128)(2,1)}, s32[64]{0:T(128)}) custom-call(s32[2,32]{1,0:T(2,128)} %bitcast.16, s32[2,32]{1,0:T(2,128)} %bitcast.17, s32[2,32]{1,0:T(2,128)} %bitcast.18, s32[2,32]{1,0:T(2,128)} %bitcast.19, bf16[64,64,128]{2,1,0:T(8,128)(2,1)} %bitcast.12), custom_call_target="tpu_custom_call" | custom-call | tf_op jit(solution)/shard_map/pack/pallas_call | solution.py:103
  3.7 15.1 %all-to-all-start = ((bf16[32,272,128]{2,1,0:T(8,128)(2,1)}), bf16[32,272,128]{2,1,0:T(8,128)(2,1)S(1)}, u32[]{:S(2)}, u32[]{:S(2)}) async-start(bf16[32,272,128]{2,1,0:T(8,128)(2,1)} %get-tuple-element.15), calls=%async_computation | async-start | bytes 4456448 | tf_op jit(solution)/shard_map/all_to_all | solution.py:445
  18.8 0.8 slice_bitcast_fusion
  19.6 3.3 %collective-permute-start = (bf16[2,64,128]{2,1,0:T(8,128)(2,1)S(1)}, bf16[2,64,128]{2,1,0:T(8,128)(2,1)S(1)}, u32[]{:S(2)}, u32[]{:S(2)}) collective-permute-start(bf16[2,64,128]{2,1,0:T(8,128)(2,1)S(1)} %get-tuple-element.27), channel_id=1, source_target_pairs={{0,1},{1,2},{2,3},{3,4},{4,5},{5,6},{6,7},{7,8},{8,9},{9,10},{10,1... | collective-permute-start | bytes 98312 | tf_op jit(solution)/shard_map/ppermute | solution.py:446
  22.9 4.6 %collective-permute-start.1 = (bf16[2,64,128]{2,1,0:T(8,128)(2,1)S(1)}, bf16[2,64,128]{2,1,0:T(8,128)(2,1)S(1)}, u32[]{:S(2)}, u32[]{:S(2)}) collective-permute-start(bf16[2,64,128]{2,1,0:T(8,128)(2,1)S(1)} %get-tuple-element.26), channel_id=1, source_target_pairs={{1,0},{2,1},{3,2},{4,3},{5,4},{6,5},{7,6},{8,7},{9,8},{10,9},{11,1... | collective-permute-start | bytes 98312 | tf_op jit(solution)/shard_map/ppermute | solution.py:447
  27.6 47.5 %collective-permute-done.before = bf16[2,64,128]{2,1,0:T(8,128)(2,1)S(1)} collective-permute-done((bf16[2,64,128]{2,1,0:T(8,128)(2,1)S(1)}, bf16[2,64,128]{2,1,0:T(8,128)(2,1)S(1)}, u32[]{:S(2)}, u32[]{:S(2)}) %collective-permute-start) | collective-permute-done | bytes 32800 | tf_op jit(solution)/shard_map/ppermute | solution.py:446
  75.0 0.0 copy-start
  75.0 0.0 collective-permute-done.1.after
  75.0 0.0 copy-start.1
  75.0 4.4 %all-to-all-done.received = bf16[32,272,128]{2,1,0:T(8,128)(2,1)S(1)} async-done(((bf16[32,272,128]{2,1,0:T(8,128)(2,1)}), bf16[32,272,128]{2,1,0:T(8,128)(2,1)S(1)}, u32[]{:S(2)}, u32[]{:S(2)}) %all-to-all-start) | async-done | bytes 2228256 | tf_op jit(solution)/shard_map/all_to_all | solution.py:445
  79.5 0.0 copy-done
  79.5 0.0 copy-done.1
  79.5 6.0 %adjoint.1 = (bf16[64,64,128]{2,1,0:T(8,128)(2,1)}, f32[4,64,128]{2,1,0:T(8,128)}, bf16[2,64,128]{2,1,0:T(8,128)(2,1)}, bf16[2,64,128]{2,1,0:T(8,128)(2,1)}, bf1...) custom-call(s32[64]{0:T(128)} %get-tuple-element.14.places_all, bf16[32,272,128]{2,1,0:T(8,128)(2,1)S(1)} %all-to-all-done.received, ...), custom_call_target="tpu_custom_call" | custom-call | tf_op jit(solution)/shard_map/adjoint/pallas_call | solution.py:301
  85.5 6.7 %all-to-all-start.1 = ((bf16[128,2,128]{2,1,0:T(2,128)(2,1)}), bf16[128,2,128]{2,1,0:T(2,128)(2,1)S(1)}, u32[]{:S(2)}, u32[]{:S(2)}) async-start(bf16[128,2,128]{2,1,0:T(2,128)(2,1)} %get-tuple-element.16), calls=%async_computation.1 | async-start | bytes 131072 | tf_op jit(solution)/shard_map/all_to_all | solution.py:451
  92.2 2.5 %collective-permute-start.2 = (bf16[2,64,128]{2,1,0:T(8,128)(2,1)}, bf16[2,64,128]{2,1,0:T(8,128)(2,1)S(1)}, u32[]{:S(2)}, u32[]{:S(2)}) collective-permute-start(bf16[2,64,128]{2,1,0:T(8,128)(2,1)} %get-tuple-element.21), channel_id=1, source_target_pairs={{0,1},{1,2},{2,3},{3,4},{4,5},{5,6},{6,7},{7,8},{8,9},{9,10},{10,1... | collective-permute-start | bytes 98312 | tf_op jit(solution)/shard_map/ppermute | solution.py:453
  94.7 5.4 %collective-permute-start.3 = (bf16[2,64,128]{2,1,0:T(8,128)(2,1)}, bf16[2,64,128]{2,1,0:T(8,128)(2,1)S(1)}, u32[]{:S(2)}, u32[]{:S(2)}) collective-permute-start(bf16[2,64,128]{2,1,0:T(8,128)(2,1)} %get-tuple-element.22), channel_id=1, source_target_pairs={{1,0},{2,1},{3,2},{4,3},{5,4},{6,5},{7,6},{8,7},{9,8},{10,9},{11,1... | collective-permute-start | bytes 98312 | tf_op jit(solution)/shard_map/ppermute | solution.py:452
  100.2 0.9 hold.1
  101.1 0.0 collective-permute-done.2.from_before
  101.1 0.9 collective-permute-done.3.from_after
  102.1 2.8 %all-to-all-done.1.returned = bf16[128,2,128]{2,1,0:T(2,128)(2,1)S(1)} async-done(((bf16[128,2,128]{2,1,0:T(2,128)(2,1)}), bf16[128,2,128]{2,1,0:T(2,128)(2,1)S(1)}, u32[]{:S(2)}, u32[]{:S(2)}) %all-to-all-start.1) | async-done | bytes 65568 | tf_op jit(solution)/shard_map/all_to_all | solution.py:451
  104.9 1.5 %finish.1 = (bf16[64,64,128]{2,1,0:T(8,128)(2,1)}, f32[64,2,128]{2,1,0:T(2,128)}) custom-call(s32[64]{0:T(128)} %get-tuple-element.14.places_all, bf16[128,2,128]{2,1,0:T(2,128)(2,1)S(1)} %all-to-all-done.1.returned, f32[64,2,128]{2,1,0:T(2,128)S(1)} %get-tuple-element.19.sensed_home, ...), custom_call_target="tpu_custom_call", output_to_operand_aliasing={{0}: (6, {})} | custom-call | tf_op jit(solution)/shard_map/finish/pallas_call | solution.py:411
Async XLA Ops:
  3.7 75.7 %all-to-all-start = ((bf16[32,272,128]{2,1,0:T(8,128)(2,1)}), bf16[32,272,128]{2,1,0:T(8,128)(2,1)S(1)}, u32[]{:S(2)}, u32[]{:S(2)}) async-start(bf16[32,272,128]{2,1,0:T(8,128)(2,1)} %get-tuple-element.15), calls=%async_computation | async-start | bytes 4456448 | tf_op jit(solution)/shard_map/all_to_all | solution.py:445
  19.6 55.4 %collective-permute-start = (bf16[2,64,128]{2,1,0:T(8,128)(2,1)S(1)}, bf16[2,64,128]{2,1,0:T(8,128)(2,1)S(1)}, u32[]{:S(2)}, u32[]{:S(2)}) collective-permute-start(bf16[2,64,128]{2,1,0:T(8,128)(2,1)S(1)} %get-tuple-element.27), channel_id=1, source_target_pairs={{0,1},{1,2},{2,3},{3,4},{4,5},{5,6},{6,7},{7,8},{8,9},{9,10},{10,1... | collective-permute-start | bytes 98312 | tf_op jit(solution)/shard_map/ppermute | solution.py:446
  22.9 52.1 %collective-permute-start.1 = (bf16[2,64,128]{2,1,0:T(8,128)(2,1)S(1)}, bf16[2,64,128]{2,1,0:T(8,128)(2,1)S(1)}, u32[]{:S(2)}, u32[]{:S(2)}) collective-permute-start(bf16[2,64,128]{2,1,0:T(8,128)(2,1)S(1)} %get-tuple-element.26), channel_id=1, source_target_pairs={{1,0},{2,1},{3,2},{4,3},{5,4},{6,5},{7,6},{8,7},{9,8},{10,9},{11,1... | collective-permute-start | bytes 98312 | tf_op jit(solution)/shard_map/ppermute | solution.py:447
  75.0 4.4 %copy-start = (bf16[2,64,128]{2,1,0:T(8,128)(2,1)}, bf16[2,64,128]{2,1,0:T(8,128)(2,1)S(1)}, u32[]{:S(2)}) copy-start(bf16[2,64,128]{2,1,0:T(8,128)(2,1)S(1)} %collective-permute-done.before) | copy-start | bytes 98308
  75.0 4.4 %copy-start.1 = (bf16[2,64,128]{2,1,0:T(8,128)(2,1)}, bf16[2,64,128]{2,1,0:T(8,128)(2,1)S(1)}, u32[]{:S(2)}) copy-start(bf16[2,64,128]{2,1,0:T(8,128)(2,1)S(1)} %collective-permute-done.1.after) | copy-start | bytes 98308
  85.5 19.3 %all-to-all-start.1 = ((bf16[128,2,128]{2,1,0:T(2,128)(2,1)}), bf16[128,2,128]{2,1,0:T(2,128)(2,1)S(1)}, u32[]{:S(2)}, u32[]{:S(2)}) async-start(bf16[128,2,128]{2,1,0:T(2,128)(2,1)} %get-tuple-element.16), calls=%async_computation.1 | async-start | bytes 131072 | tf_op jit(solution)/shard_map/all_to_all | solution.py:451
  92.2 8.9 %collective-permute-start.2 = (bf16[2,64,128]{2,1,0:T(8,128)(2,1)}, bf16[2,64,128]{2,1,0:T(8,128)(2,1)S(1)}, u32[]{:S(2)}, u32[]{:S(2)}) collective-permute-start(bf16[2,64,128]{2,1,0:T(8,128)(2,1)} %get-tuple-element.21), channel_id=1, source_target_pairs={{0,1},{1,2},{2,3},{3,4},{4,5},{5,6},{6,7},{7,8},{8,9},{9,10},{10,1... | collective-permute-start | bytes 98312 | tf_op jit(solution)/shard_map/ppermute | solution.py:453
  94.7 7.3 %collective-permute-start.3 = (bf16[2,64,128]{2,1,0:T(8,128)(2,1)}, bf16[2,64,128]{2,1,0:T(8,128)(2,1)S(1)}, u32[]{:S(2)}, u32[]{:S(2)}) collective-permute-start(bf16[2,64,128]{2,1,0:T(8,128)(2,1)} %get-tuple-element.22), channel_id=1, source_target_pairs={{1,0},{2,1},{3,2},{4,3},{5,4},{6,5},{7,6},{8,7},{9,8},{10,9},{11,1... | collective-permute-start | bytes 98312 | tf_op jit(solution)/shard_map/ppermute | solution.py:452

commit v5 on v4

--- a/solution.py
+++ b/solution.py
@@ -27,27 +27,65 @@
 
 def pack_kernel(
     owner_all, step_all, column_all, kind_all, adjoint, send, places,
-    owner, step, column, kind, codes, counts, tiles, meta, load_sem, sem, meta_sem,
+    owner, step, column, kind, counts, rows, tiles, meta, list_sem, load_sem, sem, meta_sem,
 ):
     tile_cols, tile_rows = owner.shape
     tiles_here, levels, _ = adjoint.shape
     lon_count = counts.shape[0]
     me = lax.axis_index("lon")
+    wholes = (owner_all, step_all, column_all, kind_all)
+    lists = [
+        pltpu.make_async_copy(whole, rows.at[n], list_sem.at[n]) for n, whole in enumerate(wholes)
+    ]
     asks = [
         pltpu.make_async_copy(whole, here, load_sem.at[n])
-        for n, (whole, here) in enumerate(
-            ((owner_all, owner), (step_all, step), (column_all, column), (kind_all, kind))
-        )
+        for n, (whole, here) in enumerate(zip(wholes, (owner, step, column, kind)))
     ]
-    for ask in asks:
+    for ask in lists + asks:
         ask.start()
     load = pltpu.make_async_copy(adjoint, tiles, load_sem.at[len(asks)])
     load.start()
 
     for d in range(lon_count):
         counts[d] = 0
-        for r in range(CAP):
-            codes[d * CAP + r] = 0
+    for ask in lists:
+        ask.wait()
+
+    wide = (lon_count, tile_rows)
+    device = lax.broadcasted_iota(jnp.int32, wide, 0)
+    named, asked = [], []
+    for j in range(tile_cols):
+        to = jnp.broadcast_to(rows[0, j : j + 1, :], wide)
+        block = (lax.broadcasted_iota(jnp.int32, (1, tile_rows), 1) + rows[1, j : j + 1, :]) * tile_cols
+        code = (block + rows[2, j : j + 1, :]) * KINDS + rows[3, j : j + 1, :] + 1
+        named.append((to == device) & (to != me))
+        asked.append(jnp.broadcast_to(code, wide))
+    square = (tile_rows, tile_rows)
+    earlier = lax.broadcasted_iota(jnp.int32, square, 0) < lax.broadcasted_iota(jnp.int32, square, 1)
+    in_row = sum(n.astype(jnp.float32) for n in named)
+    rank = jnp.dot(
+        in_row.astype(jnp.bfloat16), earlier.astype(jnp.bfloat16), preferred_element_type=jnp.float32
+    ).astype(jnp.int32)
+    lane = lax.broadcasted_iota(jnp.int32, (lon_count, meta.shape[2]), 1)
+    spread = jnp.zeros(lane.shape, jnp.float32)
+    ranks = []
+    for j in range(tile_cols):
+        ranks.append(rank)
+        rank = rank + named[j].astype(jnp.int32)
+    for r in range(CAP):
+        of_rank = sum(
+            jnp.where(named[j] & (ranks[j] == r), asked[j], 0).astype(jnp.float32) for j in range(tile_cols)
+        )
+        of_rank = jnp.sum(of_rank, axis=1, keepdims=True)
+        spread = jnp.where(lane % CAP == r, of_rank, spread)
+    mine = lane // CAP == lax.broadcasted_iota(jnp.int32, lane.shape, 0)
+    line = jnp.sum(jnp.where(mine, spread, 0.0), axis=0, keepdims=True)
+    line = jnp.where(line > EXACT, EXACT - line, line)
+    line = jnp.broadcast_to(line, (META, meta.shape[2])).astype(jnp.bfloat16)
+    for d in range(lon_count):
+        meta[d] = line
+    told = pltpu.make_async_copy(meta, send.at[:, pl.ds(CAP * levels, META), :], meta_sem)
+    told.start()
     for ask in asks:
         ask.wait()
     load.wait()
@@ -64,7 +102,6 @@
                 code = ((i + step[j, i]) * tile_cols + column[j, i]) * KINDS + kind[j, i] + 1
                 slot = to * CAP + rank
                 places[tile] = jnp.where(remote, slot, -code)
-                codes[jnp.where(remote, slot, me * CAP)] = jnp.where(remote, code, 0)
 
                 @pl.when(remote)
                 def _():
@@ -75,19 +112,6 @@
         return sent
 
     sent = lax.fori_loop(0, tile_rows // 4, send_rows, 0)
-    lane = lax.broadcasted_iota(jnp.int32, (8, meta.shape[2]), 1)
-    lines = [jnp.zeros(lane.shape, jnp.int32)] * CAP
-    for d in range(lon_count):
-        for r in range(CAP):
-            lines[r] = jnp.where(lane == d * CAP + r, codes[d * CAP + r], lines[r])
-    line = sum(lines[1:], lines[0])
-    line = jnp.where(line > EXACT, EXACT - line, line).astype(jnp.float32)
-    line = jnp.concatenate([line, line], axis=0).astype(jnp.bfloat16)
-    for d in range(lon_count):
-        meta[d] = line
-    told = pltpu.make_async_copy(meta, send.at[:, pl.ds(CAP * levels, META), :], meta_sem)
-    told.start()
-
     def settle(_, carry):
         pltpu.make_async_copy(tiles.at[0], send.at[0, pl.ds(0, levels), :], sem).wait()
         return carry
@@ -113,10 +137,11 @@
             pltpu.SMEM(owner.shape, jnp.int32),
             pltpu.SMEM(owner.shape, jnp.int32),
             pltpu.SMEM(owner.shape, jnp.int32),
-            pltpu.SMEM((lon_count * CAP,), jnp.int32),
             pltpu.SMEM((lon_count,), jnp.int32),
+            pltpu.VMEM((4,) + owner.shape, jnp.int32),
             pltpu.VMEM((tiles_here, levels, width), jnp.bfloat16),
             pltpu.VMEM((lon_count, META, width), jnp.bfloat16),
+            pltpu.SemaphoreType.DMA((4,)),
             pltpu.SemaphoreType.DMA((5,)),
             pltpu.SemaphoreType.DMA,
             pltpu.SemaphoreType.DMA,
@@ -370,8 +395,9 @@
 def finish_kernel(
     places_all, returned, sensed_home, own, from_before, from_after, _, result, sensed, edges, out, places, sem
 ):
-    where = pltpu.make_async_copy(places_all, places, sem.at[3])
+    where = pltpu.make_async_copy(places_all, places, sem.at[4])
     where.start()
+    half = sensed.shape[0] // 2
     tiles_here = sensed.shape[0]
     tile_cols = from_before.shape[0]
     for c in range(tile_cols):
@@ -384,7 +410,10 @@
             result.at[pl.ds(tiles_here - tile_cols, tile_cols)],
             sem.at[1],
         ),
-        pltpu.make_async_copy(out, sensed, sem.at[2]),
+        *[
+            pltpu.make_async_copy(out.at[pl.ds(h * half, half)], sensed.at[pl.ds(h * half, half)], sem.at[2 + h])
+            for h in range(2)
+        ],
     ]
     copies[0].start()
     copies[1].start()
@@ -397,8 +426,9 @@
             out[t] = jnp.where(place < 0, sensed_home[t], returned[jnp.maximum(place, 0)].astype(jnp.float32))
         return carry
 
-    lax.fori_loop(0, tiles_here // 8, place_some, 0)
-    copies[2].start()
+    for h in range(2):
+        lax.fori_loop(h * half // 8, (h + 1) * half // 8, place_some, 0)
+        copies[2 + h].start()
     for copy in copies:
         copy.wait()
 
@@ -420,7 +450,7 @@
             pltpu.VMEM((2 * tile_cols, levels, width), jnp.bfloat16),
             pltpu.VMEM((tiles_here, 2, width), jnp.float32),
             pltpu.SMEM((tiles_here,), jnp.int32),
-            pltpu.SemaphoreType.DMA((4,)),
+            pltpu.SemaphoreType.DMA((5,)),
         ],
         input_output_aliases={6: 0},
         compiler_params=pltpu.CompilerParams(vmem_limit_bytes=8 * 1024 * 1024),

time: 107 us -> 107 us (level)
  starting transfers between devices: 37.6 us -> 36.5 us
    all_to_all x1, starting transfers between devices: 6.67 us -> 5.49 us  [on_device(): lax.all_to_all(sensed_remote, 'lon', split_axis=0, concat_axis=0, tiled=T...]
    pallas_call x1, Pallas kernels: 6.05 us -> 7.2 us  [adjoint_step(): pl.pallas_call(adjoint_kernel, out_shape=(pltpu.HBM((tiles_here, levels,...]
where the time goes in v5:
time: 107 us; the launch traced here: 106 us
  waiting for transfers between devices  55.7 us (52%)
  starting transfers between devices  36.5 us (34%)
  Pallas kernels  12.6 us (12%)
    ppermute x1, waiting for transfers between devices, on_device(): before = lax.ppermute(old[-tile_cols:], 'lat', north_to_south)  47.5 us
    all_to_all x1, starting transfers between devices, on_device(): lax.all_to_all(send, 'lon', split_axis=0, concat_axis=0, tiled=True)  15.1 us
    pallas_call x1, Pallas kernels, adjoint_step(): pl.pallas_call(adjoint_kernel, out_shape=(pltpu.HBM((tiles_here, levels,...  7.2 us
    all_to_all x1, starting transfers between devices, on_device(): lax.all_to_all(sensed_remote, 'lon', split_axis=0, concat_axis=0, tiled=T...  5.49 us
    ppermute x1, starting transfers between devices, on_device(): from_after = lax.ppermute(cross_before, 'lat', south_to_north)  5.45 us
    ppermute x1, starting transfers between devices, on_device(): after = lax.ppermute(old[:tile_cols], 'lat', south_to_north)  4.63 us
    all_to_all x1, waiting for transfers between devices, on_device(): lax.all_to_all(send, 'lon', split_axis=0, concat_axis=0, tiled=True)  4.42 us
    ppermute x1, starting transfers between devices, on_device(): before = lax.ppermute(old[-tile_cols:], 'lat', north_to_south)  3.31 us
  transfers between devices with their start and end apart: 6, of which 4 were waited for; matrix products, arithmetic and copies ran while one was open for 1% of the time, Pallas kernels for 1%

profile of v5, /device:TPU:8, one launch (start us, length us, event | category | flops | bytes accessed | tf_op | source)
XLA Modules:
  0.0 106.2 jit_solution(17858982873905684939)
XLA Ops:
  0.6 2.9 %pack.1 = (bf16[32,272,128]{2,1,0:T(8,128)(2,1)}, s32[64]{0:T(128)}) custom-call(s32[2,32]{1,0:T(2,128)} %bitcast.16, s32[2,32]{1,0:T(2,128)} %bitcast.17, s32[2,32]{1,0:T(2,128)} %bitcast.18, s32[2,32]{1,0:T(2,128)} %bitcast.19, bf16[64,64,128]{2,1,0:T(8,128)(2,1)} %bitcast.12), custom_call_target="tpu_custom_call" | custom-call | tf_op jit(solution)/shard_map/pack/pallas_call | solution.py:127
  3.6 15.1 %all-to-all-start = ((bf16[32,272,128]{2,1,0:T(8,128)(2,1)}), bf16[32,272,128]{2,1,0:T(8,128)(2,1)S(1)}, u32[]{:S(2)}, u32[]{:S(2)}) async-start(bf16[32,272,128]{2,1,0:T(8,128)(2,1)} %get-tuple-element.15), calls=%async_computation | async-start | bytes 4456448 | tf_op jit(solution)/shard_map/all_to_all | solution.py:475
  18.7 0.8 slice_bitcast_fusion
  19.4 3.3 %collective-permute-start = (bf16[2,64,128]{2,1,0:T(8,128)(2,1)S(1)}, bf16[2,64,128]{2,1,0:T(8,128)(2,1)S(1)}, u32[]{:S(2)}, u32[]{:S(2)}) collective-permute-start(bf16[2,64,128]{2,1,0:T(8,128)(2,1)S(1)} %get-tuple-element.27), channel_id=1, source_target_pairs={{0,1},{1,2},{2,3},{3,4},{4,5},{5,6},{6,7},{7,8},{8,9},{9,10},{10,1... | collective-permute-start | bytes 98312 | tf_op jit(solution)/shard_map/ppermute | solution.py:476
  22.8 4.6 %collective-permute-start.1 = (bf16[2,64,128]{2,1,0:T(8,128)(2,1)S(1)}, bf16[2,64,128]{2,1,0:T(8,128)(2,1)S(1)}, u32[]{:S(2)}, u32[]{:S(2)}) collective-permute-start(bf16[2,64,128]{2,1,0:T(8,128)(2,1)S(1)} %get-tuple-element.26), channel_id=1, source_target_pairs={{1,0},{2,1},{3,2},{4,3},{5,4},{6,5},{7,6},{8,7},{9,8},{10,9},{11,1... | collective-permute-start | bytes 98312 | tf_op jit(solution)/shard_map/ppermute | solution.py:477
  27.4 47.5 %collective-permute-done.before = bf16[2,64,128]{2,1,0:T(8,128)(2,1)S(1)} collective-permute-done((bf16[2,64,128]{2,1,0:T(8,128)(2,1)S(1)}, bf16[2,64,128]{2,1,0:T(8,128)(2,1)S(1)}, u32[]{:S(2)}, u32[]{:S(2)}) %collective-permute-start) | collective-permute-done | bytes 32800 | tf_op jit(solution)/shard_map/ppermute | solution.py:476
  74.9 0.0 copy-start
  74.9 0.0 collective-permute-done.1.after
  74.9 0.0 copy-start.1
  74.9 4.4 %all-to-all-done.received = bf16[32,272,128]{2,1,0:T(8,128)(2,1)S(1)} async-done(((bf16[32,272,128]{2,1,0:T(8,128)(2,1)}), bf16[32,272,128]{2,1,0:T(8,128)(2,1)S(1)}, u32[]{:S(2)}, u32[]{:S(2)}) %all-to-all-start) | async-done | bytes 2228256 | tf_op jit(solution)/shard_map/all_to_all | solution.py:475
  79.3 0.0 copy-done
  79.3 0.0 copy-done.1
  79.4 7.2 %adjoint.1 = (bf16[64,64,128]{2,1,0:T(8,128)(2,1)}, f32[4,64,128]{2,1,0:T(8,128)}, bf16[2,64,128]{2,1,0:T(8,128)(2,1)}, bf16[2,64,128]{2,1,0:T(8,128)(2,1)}, bf1...) custom-call(s32[64]{0:T(128)} %get-tuple-element.14.places_all, bf16[32,272,128]{2,1,0:T(8,128)(2,1)S(1)} %all-to-all-done.received, ...), custom_call_target="tpu_custom_call" | custom-call | tf_op jit(solution)/shard_map/adjoint/pallas_call | solution.py:326
  86.6 5.5 %all-to-all-start.1 = ((bf16[128,2,128]{2,1,0:T(2,128)(2,1)}), bf16[128,2,128]{2,1,0:T(2,128)(2,1)S(1)}, u32[]{:S(2)}, u32[]{:S(2)}) async-start(bf16[128,2,128]{2,1,0:T(2,128)(2,1)} %get-tuple-element.16), calls=%async_computation.1 | async-start | bytes 131072 | tf_op jit(solution)/shard_map/all_to_all | solution.py:481
  92.1 2.5 %collective-permute-start.2 = (bf16[2,64,128]{2,1,0:T(8,128)(2,1)}, bf16[2,64,128]{2,1,0:T(8,128)(2,1)S(1)}, u32[]{:S(2)}, u32[]{:S(2)}) collective-permute-start(bf16[2,64,128]{2,1,0:T(8,128)(2,1)} %get-tuple-element.21), channel_id=1, source_target_pairs={{0,1},{1,2},{2,3},{3,4},{4,5},{5,6},{6,7},{7,8},{8,9},{9,10},{10,1... | collective-permute-start | bytes 98312 | tf_op jit(solution)/shard_map/ppermute | solution.py:483
  94.6 5.5 %collective-permute-start.3 = (bf16[2,64,128]{2,1,0:T(8,128)(2,1)}, bf16[2,64,128]{2,1,0:T(8,128)(2,1)S(1)}, u32[]{:S(2)}, u32[]{:S(2)}) collective-permute-start(bf16[2,64,128]{2,1,0:T(8,128)(2,1)} %get-tuple-element.22), channel_id=1, source_target_pairs={{1,0},{2,1},{3,2},{4,3},{5,4},{6,5},{7,6},{8,7},{9,8},{10,9},{11,1... | collective-permute-start | bytes 98312 | tf_op jit(solution)/shard_map/ppermute | solution.py:482
  100.0 0.9 hold.1
  101.0 0.0 collective-permute-done.2.from_before
  101.0 0.9 collective-permute-done.3.from_after
  101.9 2.8 %all-to-all-done.1.returned = bf16[128,2,128]{2,1,0:T(2,128)(2,1)S(1)} async-done(((bf16[128,2,128]{2,1,0:T(2,128)(2,1)}), bf16[128,2,128]{2,1,0:T(2,128)(2,1)S(1)}, u32[]{:S(2)}, u32[]{:S(2)}) %all-to-all-start.1) | async-done | bytes 65568 | tf_op jit(solution)/shard_map/all_to_all | solution.py:481
  104.7 1.5 %finish.1 = (bf16[64,64,128]{2,1,0:T(8,128)(2,1)}, f32[64,2,128]{2,1,0:T(2,128)}) custom-call(s32[64]{0:T(128)} %get-tuple-element.14.places_all, bf16[128,2,128]{2,1,0:T(2,128)(2,1)S(1)} %all-to-all-done.1.returned, f32[64,2,128]{2,1,0:T(2,128)S(1)} %get-tuple-element.19.sensed_home, ...), custom_call_target="tpu_custom_call", output_to_operand_aliasing={{0}: (6, {})} | custom-call | tf_op jit(solution)/shard_map/finish/pallas_call | solution.py:441
Async XLA Ops:
  3.6 75.8 %all-to-all-start = ((bf16[32,272,128]{2,1,0:T(8,128)(2,1)}), bf16[32,272,128]{2,1,0:T(8,128)(2,1)S(1)}, u32[]{:S(2)}, u32[]{:S(2)}) async-start(bf16[32,272,128]{2,1,0:T(8,128)(2,1)} %get-tuple-element.15), calls=%async_computation | async-start | bytes 4456448 | tf_op jit(solution)/shard_map/all_to_all | solution.py:475
  19.4 55.5 %collective-permute-start = (bf16[2,64,128]{2,1,0:T(8,128)(2,1)S(1)}, bf16[2,64,128]{2,1,0:T(8,128)(2,1)S(1)}, u32[]{:S(2)}, u32[]{:S(2)}) collective-permute-start(bf16[2,64,128]{2,1,0:T(8,128)(2,1)S(1)} %get-tuple-element.27), channel_id=1, source_target_pairs={{0,1},{1,2},{2,3},{3,4},{4,5},{5,6},{6,7},{7,8},{8,9},{9,10},{10,1... | collective-permute-start | bytes 98312 | tf_op jit(solution)/shard_map/ppermute | solution.py:476
  22.8 52.2 %collective-permute-start.1 = (bf16[2,64,128]{2,1,0:T(8,128)(2,1)S(1)}, bf16[2,64,128]{2,1,0:T(8,128)(2,1)S(1)}, u32[]{:S(2)}, u32[]{:S(2)}) collective-permute-start(bf16[2,64,128]{2,1,0:T(8,128)(2,1)S(1)} %get-tuple-element.26), channel_id=1, source_target_pairs={{1,0},{2,1},{3,2},{4,3},{5,4},{6,5},{7,6},{8,7},{9,8},{10,9},{11,1... | collective-permute-start | bytes 98312 | tf_op jit(solution)/shard_map/ppermute | solution.py:477
  74.9 4.4 %copy-start = (bf16[2,64,128]{2,1,0:T(8,128)(2,1)}, bf16[2,64,128]{2,1,0:T(8,128)(2,1)S(1)}, u32[]{:S(2)}) copy-start(bf16[2,64,128]{2,1,0:T(8,128)(2,1)S(1)} %collective-permute-done.before) | copy-start | bytes 98308
  74.9 4.4 %copy-start.1 = (bf16[2,64,128]{2,1,0:T(8,128)(2,1)}, bf16[2,64,128]{2,1,0:T(8,128)(2,1)S(1)}, u32[]{:S(2)}) copy-start(bf16[2,64,128]{2,1,0:T(8,128)(2,1)S(1)} %collective-permute-done.1.after) | copy-start | bytes 98308
  86.6 18.2 %all-to-all-start.1 = ((bf16[128,2,128]{2,1,0:T(2,128)(2,1)}), bf16[128,2,128]{2,1,0:T(2,128)(2,1)S(1)}, u32[]{:S(2)}, u32[]{:S(2)}) async-start(bf16[128,2,128]{2,1,0:T(2,128)(2,1)} %get-tuple-element.16), calls=%async_computation.1 | async-start | bytes 131072 | tf_op jit(solution)/shard_map/all_to_all | solution.py:481
  92.1 8.9 %collective-permute-start.2 = (bf16[2,64,128]{2,1,0:T(8,128)(2,1)}, bf16[2,64,128]{2,1,0:T(8,128)(2,1)S(1)}, u32[]{:S(2)}, u32[]{:S(2)}) collective-permute-start(bf16[2,64,128]{2,1,0:T(8,128)(2,1)} %get-tuple-element.21), channel_id=1, source_target_pairs={{0,1},{1,2},{2,3},{3,4},{4,5},{5,6},{6,7},{7,8},{8,9},{9,10},{10,1... | collective-permute-start | bytes 98312 | tf_op jit(solution)/shard_map/ppermute | solution.py:483
  94.6 7.4 %collective-permute-start.3 = (bf16[2,64,128]{2,1,0:T(8,128)(2,1)}, bf16[2,64,128]{2,1,0:T(8,128)(2,1)S(1)}, u32[]{:S(2)}, u32[]{:S(2)}) collective-permute-start(bf16[2,64,128]{2,1,0:T(8,128)(2,1)} %get-tuple-element.22), channel_id=1, source_target_pairs={{1,0},{2,1},{3,2},{4,3},{5,4},{6,5},{7,6},{8,7},{9,8},{10,9},{11,1... | collective-permute-start | bytes 98312 | tf_op jit(solution)/shard_map/ppermute | solution.py:482

commit v6 on v5

--- a/solution.py
+++ b/solution.py
@@ -12,7 +12,8 @@
 KINDS = 4
 CODES = 512
 EXACT = 200
-UNROLL = 12
+UNROLL = 16
+REST = 4
 PARTS = 4
 VMEM_LIMIT = 24 * 1024 * 1024
 
@@ -258,12 +259,12 @@
         source = [sources[jnp.minimum(b, block_count - 1)] for b in block]
         spread = jnp.dot(jnp.concatenate(arrived, axis=0), back[kind], preferred_element_type=jnp.float32)
         slope = jnp.dot(jnp.concatenate(source, axis=0), slopes[kind], preferred_element_type=jnp.float32)
-        for u in range(UNROLL):
+        for u in range(len(entries)):
             full = arrived[u].astype(jnp.float32)
             s = slope[u * levels : (u + 1) * levels]
             both = [jnp.sum(full * part, axis=0, keepdims=True) for part in (s[:, :width], s[:, width:])]
             sensed[place[u]] = jnp.concatenate(both, axis=0).astype(sensed.dtype)
-        for u in range(UNROLL):
+        for u in range(len(entries)):
             s = spread[u * levels : (u + 1) * levels]
             sums[block[u]] += s.astype(jnp.bfloat16).astype(jnp.float32)
 
@@ -275,12 +276,14 @@
             loads[3].wait()
         for kind in range(KINDS):
 
-            def step(n, carry, kind=kind, listing=listing, tile_at=tile_at, sensed=sensed):
-                entries = [listing[kind * room + n * UNROLL + u] for u in range(UNROLL)]
+            def step(n, first, kind=kind, listing=listing, tile_at=tile_at, sensed=sensed, wide=UNROLL):
+                entries = [listing[kind * room + first + u] for u in range(wide)]
                 some_tiles(kind, entries, tile_at, sensed)
-                return carry
-
-            lax.fori_loop(0, (many[kind] + UNROLL - 1) // UNROLL, step, 0)
+                return first + wide
+
+            done = lax.fori_loop(0, many[kind] // UNROLL, step, 0)
+            rest = (many[kind] - done + REST - 1) // REST
+            lax.fori_loop(0, rest, functools.partial(step, wide=REST), done)
 
     copies = []
 

time: 107 us -> 107 us (level)
  the two profiles are of different devices: /device:TPU:8 before, /device:TPU:10 now
where the time goes in v6:
time: 107 us
  waiting for transfers between devices  59.6 us (56%)
  starting transfers between devices  33.1 us (31%)
  Pallas kernels  12.7 us (12%)
    all_to_all x1, waiting for transfers between devices, on_device(): lax.all_to_all(send, 'lon', split_axis=0, concat_axis=0, tiled=True)  50.6 us
    all_to_all x1, starting transfers between devices, on_device(): lax.all_to_all(send, 'lon', split_axis=0, concat_axis=0, tiled=True)  15.1 us
    pallas_call x1, Pallas kernels, adjoint_step(): pl.pallas_call(adjoint_kernel, out_shape=(pltpu.HBM((tiles_here, levels,...  7.4 us
    all_to_all x1, starting transfers between devices, on_device(): lax.all_to_all(sensed_remote, 'lon', split_axis=0, concat_axis=0, tiled=T...  6.31 us
    all_to_all x1, waiting for transfers between devices, on_device(): lax.all_to_all(sensed_remote, 'lon', split_axis=0, concat_axis=0, tiled=T...  3.64 us
    ppermute x1, starting transfers between devices, on_device(): before = lax.ppermute(old[-tile_cols:], 'lat', north_to_south)  3.34 us
    ppermute x1, waiting for transfers between devices, on_device(): after = lax.ppermute(old[:tile_cols], 'lat', south_to_north)  3.29 us
    ppermute x1, starting transfers between devices, on_device(): from_after = lax.ppermute(cross_before, 'lat', south_to_north)  2.94 us
  transfers between devices with their start and end apart: 6, of which 4 were waited for; matrix products, arithmetic and copies ran while one was open for 1% of the time, Pallas kernels for 1%

profile of v6, /device:TPU:10, one launch (start us, length us, event | category | flops | bytes accessed | tf_op | source)
XLA Modules:
  0.0 106.9 jit_solution(3322647843706932930)
XLA Ops:
  0.6 2.9 %pack.1 = (bf16[32,272,128]{2,1,0:T(8,128)(2,1)}, s32[64]{0:T(128)}) custom-call(s32[2,32]{1,0:T(2,128)} %bitcast.16, s32[2,32]{1,0:T(2,128)} %bitcast.17, s32[2,32]{1,0:T(2,128)} %bitcast.18, s32[2,32]{1,0:T(2,128)} %bitcast.19, bf16[64,64,128]{2,1,0:T(8,128)(2,1)} %bitcast.12), custom_call_target="tpu_custom_call" | custom-call | tf_op jit(solution)/shard_map/pack/pallas_call | solution.py:128
  3.5 15.1 %all-to-all-start = ((bf16[32,272,128]{2,1,0:T(8,128)(2,1)}), bf16[32,272,128]{2,1,0:T(8,128)(2,1)S(1)}, u32[]{:S(2)}, u32[]{:S(2)}) async-start(bf16[32,272,128]{2,1,0:T(8,128)(2,1)} %get-tuple-element.15), calls=%async_computation | async-start | bytes 4456448 | tf_op jit(solution)/shard_map/all_to_all | solution.py:478
  18.6 0.8 slice_bitcast_fusion
  19.4 3.3 %collective-permute-start = (bf16[2,64,128]{2,1,0:T(8,128)(2,1)S(1)}, bf16[2,64,128]{2,1,0:T(8,128)(2,1)S(1)}, u32[]{:S(2)}, u32[]{:S(2)}) collective-permute-start(bf16[2,64,128]{2,1,0:T(8,128)(2,1)S(1)} %get-tuple-element.27), channel_id=1, source_target_pairs={{0,1},{1,2},{2,3},{3,4},{4,5},{5,6},{6,7},{7,8},{8,9},{9,10},{10,1... | collective-permute-start | bytes 98312 | tf_op jit(solution)/shard_map/ppermute | solution.py:479
  22.7 2.5 %collective-permute-start.1 = (bf16[2,64,128]{2,1,0:T(8,128)(2,1)S(1)}, bf16[2,64,128]{2,1,0:T(8,128)(2,1)S(1)}, u32[]{:S(2)}, u32[]{:S(2)}) collective-permute-start(bf16[2,64,128]{2,1,0:T(8,128)(2,1)S(1)} %get-tuple-element.26), channel_id=1, source_target_pairs={{1,0},{2,1},{3,2},{4,3},{5,4},{6,5},{7,6},{8,7},{9,8},{10,9},{11,1... | collective-permute-start | bytes 98312 | tf_op jit(solution)/shard_map/ppermute | solution.py:480
  25.2 0.0 collective-permute-done.before
  25.2 0.0 copy-start
  25.3 3.3 %collective-permute-done.1.after = bf16[2,64,128]{2,1,0:T(8,128)(2,1)S(1)} collective-permute-done((bf16[2,64,128]{2,1,0:T(8,128)(2,1)S(1)}, bf16[2,64,128]{2,1,0:T(8,128)(2,1)S(1)}, u32[]{:S(2)}, u32[]{:S(2)}) %collective-permute-start.1) | collective-permute-done | bytes 32800 | tf_op jit(solution)/shard_map/ppermute | solution.py:480
  28.5 0.0 copy-start.1
  28.5 50.6 %all-to-all-done.received = bf16[32,272,128]{2,1,0:T(8,128)(2,1)S(1)} async-done(((bf16[32,272,128]{2,1,0:T(8,128)(2,1)}), bf16[32,272,128]{2,1,0:T(8,128)(2,1)S(1)}, u32[]{:S(2)}, u32[]{:S(2)}) %all-to-all-start) | async-done | bytes 2228256 | tf_op jit(solution)/shard_map/all_to_all | solution.py:478
  79.1 0.0 copy-done
  79.1 0.0 copy-done.1
  79.1 7.4 %adjoint.1 = (bf16[64,64,128]{2,1,0:T(8,128)(2,1)}, f32[4,64,128]{2,1,0:T(8,128)}, bf16[2,64,128]{2,1,0:T(8,128)(2,1)}, bf16[2,64,128]{2,1,0:T(8,128)(2,1)}, bf1...) custom-call(s32[64]{0:T(128)} %get-tuple-element.14.places_all, bf16[32,272,128]{2,1,0:T(8,128)(2,1)S(1)} %all-to-all-done.received, ...), custom_call_target="tpu_custom_call" | custom-call | tf_op jit(solution)/shard_map/adjoint/pallas_call | solution.py:329
  86.5 6.3 %all-to-all-start.1 = ((bf16[128,2,128]{2,1,0:T(2,128)(2,1)}), bf16[128,2,128]{2,1,0:T(2,128)(2,1)S(1)}, u32[]{:S(2)}, u32[]{:S(2)}) async-start(bf16[128,2,128]{2,1,0:T(2,128)(2,1)} %get-tuple-element.16), calls=%async_computation.1 | async-start | bytes 131072 | tf_op jit(solution)/shard_map/all_to_all | solution.py:484
  92.8 2.9 %collective-permute-start.2 = (bf16[2,64,128]{2,1,0:T(8,128)(2,1)}, bf16[2,64,128]{2,1,0:T(8,128)(2,1)S(1)}, u32[]{:S(2)}, u32[]{:S(2)}) collective-permute-start(bf16[2,64,128]{2,1,0:T(8,128)(2,1)} %get-tuple-element.21), channel_id=1, source_target_pairs={{0,1},{1,2},{2,3},{3,4},{4,5},{5,6},{6,7},{7,8},{8,9},{9,10},{10,1... | collective-permute-start | bytes 98312 | tf_op jit(solution)/shard_map/ppermute | solution.py:486
  95.8 2.9 %collective-permute-start.3 = (bf16[2,64,128]{2,1,0:T(8,128)(2,1)}, bf16[2,64,128]{2,1,0:T(8,128)(2,1)S(1)}, u32[]{:S(2)}, u32[]{:S(2)}) collective-permute-start(bf16[2,64,128]{2,1,0:T(8,128)(2,1)} %get-tuple-element.22), channel_id=1, source_target_pairs={{1,0},{2,1},{3,2},{4,3},{5,4},{6,5},{7,6},{8,7},{9,8},{10,9},{11,1... | collective-permute-start | bytes 98312 | tf_op jit(solution)/shard_map/ppermute | solution.py:485
  98.7 0.9 hold.1
  99.6 0.0 collective-permute-done.2.from_before
  99.6 2.1 %collective-permute-done.3.from_after = bf16[2,64,128]{2,1,0:T(8,128)(2,1)S(1)} collective-permute-done((bf16[2,64,128]{2,1,0:T(8,128)(2,1)}, bf16[2,64,128]{2,1,0:T(8,128)(2,1)S(1)}, u32[]{:S(2)}, u32[]{:S(2)}) %collective-permute-start.3) | collective-permute-done | bytes 32800 | tf_op jit(solution)/shard_map/ppermute | solution.py:485
  101.8 3.6 %all-to-all-done.1.returned = bf16[128,2,128]{2,1,0:T(2,128)(2,1)S(1)} async-done(((bf16[128,2,128]{2,1,0:T(2,128)(2,1)}), bf16[128,2,128]{2,1,0:T(2,128)(2,1)S(1)}, u32[]{:S(2)}, u32[]{:S(2)}) %all-to-all-start.1) | async-done | bytes 65568 | tf_op jit(solution)/shard_map/all_to_all | solution.py:484
  105.4 1.5 %finish.1 = (bf16[64,64,128]{2,1,0:T(8,128)(2,1)}, f32[64,2,128]{2,1,0:T(2,128)}) custom-call(s32[64]{0:T(128)} %get-tuple-element.14.places_all, bf16[128,2,128]{2,1,0:T(2,128)(2,1)S(1)} %all-to-all-done.1.returned, f32[64,2,128]{2,1,0:T(2,128)S(1)} %get-tuple-element.19.sensed_home, ...), custom_call_target="tpu_custom_call", output_to_operand_aliasing={{0}: (6, {})} | custom-call | tf_op jit(solution)/shard_map/finish/pallas_call | solution.py:444
Async XLA Ops:
  3.5 75.6 %all-to-all-start = ((bf16[32,272,128]{2,1,0:T(8,128)(2,1)}), bf16[32,272,128]{2,1,0:T(8,128)(2,1)S(1)}, u32[]{:S(2)}, u32[]{:S(2)}) async-start(bf16[32,272,128]{2,1,0:T(8,128)(2,1)} %get-tuple-element.15), calls=%async_computation | async-start | bytes 4456448 | tf_op jit(solution)/shard_map/all_to_all | solution.py:478
  19.4 5.8 %collective-permute-start = (bf16[2,64,128]{2,1,0:T(8,128)(2,1)S(1)}, bf16[2,64,128]{2,1,0:T(8,128)(2,1)S(1)}, u32[]{:S(2)}, u32[]{:S(2)}) collective-permute-start(bf16[2,64,128]{2,1,0:T(8,128)(2,1)S(1)} %get-tuple-element.27), channel_id=1, source_target_pairs={{0,1},{1,2},{2,3},{3,4},{4,5},{5,6},{6,7},{7,8},{8,9},{9,10},{10,1... | collective-permute-start | bytes 98312 | tf_op jit(solution)/shard_map/ppermute | solution.py:479
  22.7 5.8 %collective-permute-start.1 = (bf16[2,64,128]{2,1,0:T(8,128)(2,1)S(1)}, bf16[2,64,128]{2,1,0:T(8,128)(2,1)S(1)}, u32[]{:S(2)}, u32[]{:S(2)}) collective-permute-start(bf16[2,64,128]{2,1,0:T(8,128)(2,1)S(1)} %get-tuple-element.26), channel_id=1, source_target_pairs={{1,0},{2,1},{3,2},{4,3},{5,4},{6,5},{7,6},{8,7},{9,8},{10,9},{11,1... | collective-permute-start | bytes 98312 | tf_op jit(solution)/shard_map/ppermute | solution.py:480
  25.2 53.9 %copy-start = (bf16[2,64,128]{2,1,0:T(8,128)(2,1)}, bf16[2,64,128]{2,1,0:T(8,128)(2,1)S(1)}, u32[]{:S(2)}) copy-start(bf16[2,64,128]{2,1,0:T(8,128)(2,1)S(1)} %collective-permute-done.before) | copy-start | bytes 98308
  28.5 50.6 %copy-start.1 = (bf16[2,64,128]{2,1,0:T(8,128)(2,1)}, bf16[2,64,128]{2,1,0:T(8,128)(2,1)S(1)}, u32[]{:S(2)}) copy-start(bf16[2,64,128]{2,1,0:T(8,128)(2,1)S(1)} %collective-permute-done.1.after) | copy-start | bytes 98308
  86.5 18.9 %all-to-all-start.1 = ((bf16[128,2,128]{2,1,0:T(2,128)(2,1)}), bf16[128,2,128]{2,1,0:T(2,128)(2,1)S(1)}, u32[]{:S(2)}, u32[]{:S(2)}) async-start(bf16[128,2,128]{2,1,0:T(2,128)(2,1)} %get-tuple-element.16), calls=%async_computation.1 | async-start | bytes 131072 | tf_op jit(solution)/shard_map/all_to_all | solution.py:484
  92.8 6.8 %collective-permute-start.2 = (bf16[2,64,128]{2,1,0:T(8,128)(2,1)}, bf16[2,64,128]{2,1,0:T(8,128)(2,1)S(1)}, u32[]{:S(2)}, u32[]{:S(2)}) collective-permute-start(bf16[2,64,128]{2,1,0:T(8,128)(2,1)} %get-tuple-element.21), channel_id=1, source_target_pairs={{0,1},{1,2},{2,3},{3,4},{4,5},{5,6},{6,7},{7,8},{8,9},{9,10},{10,1... | collective-permute-start | bytes 98312 | tf_op jit(solution)/shard_map/ppermute | solution.py:486
  95.8 6.0 %collective-permute-start.3 = (bf16[2,64,128]{2,1,0:T(8,128)(2,1)}, bf16[2,64,128]{2,1,0:T(8,128)(2,1)S(1)}, u32[]{:S(2)}, u32[]{:S(2)}) collective-permute-start(bf16[2,64,128]{2,1,0:T(8,128)(2,1)} %get-tuple-element.22), channel_id=1, source_target_pairs={{1,0},{2,1},{3,2},{4,3},{5,4},{6,5},{7,6},{8,7},{9,8},{10,9},{11,1... | collective-permute-start | bytes 98312 | tf_op jit(solution)/shard_map/ppermute | solution.py:485
